TPU v7x, 512 devices: a whole 4x4x16 slice. The times are simulated.
512 devices in a mesh: gx: 8 (over z_lo), gy: 8 (over x, z_hi), gz: 8 (over y, core).
Axes of the slice: x: 4, y: 4, z: 16 (z_hi: 2, z_lo: 8; z = z_hi * 8 + z_lo), core: 2. Of those that a mesh axis runs over, the one named last changes fastest.
Arguments:
- inputs: bfloat16 [2048, 12288], P('gx', 'gz'), may hold values from -6 to 6
- weight: bfloat16 [12288, 24576], P(('gz', 'gx'), 'gy'), may hold values from -0.0546875 to 0.0546875
- grad_out: bfloat16 [2048, 24576], P(('gx', 'gz'), 'gy'), may hold values from -6 to 6
- pre_act: bfloat16 [2048, 24576], P(('gx', 'gz'), 'gy'), may hold values from -6 to 6
Outputs:
- grad_in: bfloat16 [2048, 12288], P('gx', 'gz')
- grad_weight: bfloat16 [12288, 24576], P(('gz', 'gx'), 'gy')
All inputs are finite; a program needn't handle non-finite values.
Results may differ from a plain program's by a relative error of at most 0.0049.
Values may be sent and summed in bfloat16 or wider, within the bound.
No kernel may reach another device: no remote copies, remote signals or barrier semaphores. Data moves between devices by JAX's collectives and lax.ppermute only.
A program may use at most 64 MiB of HBM per device.

v0:
```python
import jax
import jax.numpy as jnp
from jax import lax
from jax.sharding import PartitionSpec as P


def gelu_slope(value):
    scale = 0.7978845608028654
    tangent = jnp.tanh(scale * (value + 0.044715 * value * value * value))
    inner = scale * (1.0 + 3.0 * 0.044715 * value * value)
    return 0.5 * (1.0 + tangent) + 0.5 * value * (1.0 - tangent * tangent) * inner


def shards(inputs, weight, grad_out, pre_act):
    grad_hidden = (grad_out.astype(jnp.float32) * gelu_slope(pre_act.astype(jnp.float32))).astype(
        jnp.bfloat16
    )
    input_cols = lax.all_to_all(inputs, "gx", split_axis=1, concat_axis=0, tiled=True)
    piece = lax.all_gather(grad_hidden, ("gx", "gz"), axis=0, tiled=True)
    weight_sum = lax.dot_general(
        input_cols, piece, (((0,), (0,)), ((), ())), preferred_element_type=jnp.float32
    )
    product = lax.dot_general(
        piece, weight, (((1,), (1,)), ((), ())), preferred_element_type=jnp.float32
    )
    input_part = product
    totals = (weight_sum, input_part)
    weight_sum, input_part = totals
    summed = lax.psum(input_part, "gy").astype(jnp.bfloat16)
    grad_in = lax.all_to_all(summed, "gx", split_axis=0, concat_axis=1, tiled=True)
    return (grad_in, weight_sum.astype(jnp.bfloat16))


def solution(mesh):
    in_specs = (P("gx", "gz"), P(("gz", "gx"), "gy"), P(("gx", "gz"), "gy"), P(("gx", "gz"), "gy"))
    out_specs = (P("gx", "gz"), P(("gz", "gx"), "gy"))
    return jax.shard_map(shards, mesh=mesh, in_specs=in_specs, out_specs=out_specs, check_vma=False)
```

profile of v0, /device:TPU:16, one launch (start us, length us, event | category | flops | bytes accessed | tf_op | source)
XLA Modules:
  0.0 525.9 jit_solution(16548408613577400167)
XLA Ops:
  7.2 0.0 copy-start
  7.2 0.0 all-gather.2.cloned.1.call-start
  7.2 2.1 fusion.7
  9.3 0.0 all-gather.2.cloned.1.call-update
  9.3 2.3 copy.8
  11.6 12.5 %all-to-all-start.1 = ((bf16[256,8,192]{0,2,1:T(8,128)(2,1)}), bf16[256,8,192]{0,2,1:T(8,128)(2,1)S(1)}, u32[]{:S(2)}, u32[]{:S(2)}) async-start(bf16[256,8,192]{0,2,1:T(8,128)(2,1)} %bitcast.2), calls=%async_computation.1 | async-start | bytes 1572864 | tf_op jit(solution)/shard_map/all_to_all | solution.py:18
  24.1 143.9 %all-gather.2.cloned.1.call-done = bf16[2048,3072]{1,0:T(8,128)(2,1)} async-done(((bf16[32,3072]{1,0:T(8,128)(2,1)}), bf16[2048,3072]{1,0:T(8,128)(2,1)}) %all-gather.2.cloned.1.call-update) | async-done | bytes 12582928 | tf_op jit(solution)/shard_map/all_gather | solution.py:19
  168.0 0.0 copy-done
  168.0 10.0 %fusion.10 = f32[2048,192]{0,1:T(8,128)} fusion(bf16[2048,3072]{1,0:T(8,128)(2,1)} %all-gather.2.cloned.1.call-done, bf16[192,3072]{1,0:T(8,128)(2,1)S(1)} %copy-done), kind=kOutput, calls=%fused_computation.19 | convolution fusion | flops 2415919104 | bytes 15335424 | tf_op jit(solution)/shard_map/dot_general | solution.py:23
  178.0 281.4 %all-reduce.1 = bf16[2048,192]{0,1:T(8,128)(2,1)S(1)} all-reduce(f32[2048,192]{0,1:T(8,128)} %fusion.10), channel_id=1, replica_groups=mesh['gx'=8,'gy'=8,'gz'=8] {'gy'}, use_global_device_ids=true, to_apply=%region_0.0 | all-reduce | flops 393216 | bytes 2359296 | tf_op jit(solution)/shard_map/psum | solution.py:29
  459.4 0.9 copy.14
  460.4 0.0 all-to-all-done.1
  460.4 19.8 %all-to-all-start = ((bf16[8,256,192]{1,2,0:T(8,128)(2,1)}), bf16[8,256,192]{1,2,0:T(8,128)(2,1)S(1)}, u32[]{:S(2)}, u32[]{:S(2)}) async-start(bf16[8,256,192]{1,2,0:T(8,128)(2,1)} %bitcast.16), calls=%async_computation | async-start | bytes 1572864 | tf_op jit(solution)/shard_map/all_to_all | solution.py:30
  480.2 0.1 copy.12
  480.3 8.2 %fusion = bf16[192,3072]{1,0:T(8,128)(2,1)} fusion(bf16[2048,192]{0,1:T(8,128)(2,1)S(1)} %bitcast.20, bf16[2048,3072]{1,0:T(8,128)(2,1)} %all-gather.2.cloned.1.call-done), kind=kOutput, calls=%fused_computation.1 | convolution fusion | flops 2416508928 | bytes 14548992 | tf_op jit(solution)/shard_map/dot_general | solution.py:20
  488.6 29.3 %all-to-all-done = bf16[8,256,192]{1,2,0:T(8,128)(2,1)S(1)} async-done(((bf16[8,256,192]{1,2,0:T(8,128)(2,1)}), bf16[8,256,192]{1,2,0:T(8,128)(2,1)S(1)}, u32[]{:S(2)}, u32[]{:S(2)}) %all-to-all-start) | async-done | bytes 786464 | tf_op jit(solution)/shard_map/all_to_all | solution.py:30
  517.9 1.2 copy.10
Async XLA Ops:
  7.2 160.8 %copy-start = (bf16[192,3072]{1,0:T(8,128)(2,1)S(1)}, bf16[192,3072]{1,0:T(8,128)(2,1)}, u32[]{:S(2)}) copy-start(bf16[192,3072]{1,0:T(8,128)(2,1)} %param.5) | copy-start | bytes 3538948
  7.2 160.8 %all-gather.2.cloned.1.call-start = ((), (), s32[]{:S(2)}) async-start(), calls=%async_computation.2 | async-start | bytes 12779520 | tf_op jit(solution)/shard_map/all_gather | solution.py:19
  11.6 448.8 %all-to-all-start.1 = ((bf16[256,8,192]{0,2,1:T(8,128)(2,1)}), bf16[256,8,192]{0,2,1:T(8,128)(2,1)S(1)}, u32[]{:S(2)}, u32[]{:S(2)}) async-start(bf16[256,8,192]{0,2,1:T(8,128)(2,1)} %bitcast.2), calls=%async_computation.1 | async-start | bytes 1572864 | tf_op jit(solution)/shard_map/all_to_all | solution.py:18
  460.4 57.5 %all-to-all-start = ((bf16[8,256,192]{1,2,0:T(8,128)(2,1)}), bf16[8,256,192]{1,2,0:T(8,128)(2,1)S(1)}, u32[]{:S(2)}, u32[]{:S(2)}) async-start(bf16[8,256,192]{1,2,0:T(8,128)(2,1)} %bitcast.16), calls=%async_computation | async-start | bytes 1572864 | tf_op jit(solution)/shard_map/all_to_all | solution.py:30
Sparse Core Ops, SparseCore 0:
  10.7 157.1 all-gather.1
where the time goes:
time: 526 us
  blocking collectives  281 us (53%)
  waiting for transfers between devices  173 us (33%)
  starting transfers between devices  32.4 us (6%)
  matrix products  18.3 us (3%)
  between operations  14.1 us (3%)
    psum x1, blocking collectives, shards(): summed = lax.psum(input_part, 'gy').astype(jnp.bfloat16)  281 us
    all_gather x1, waiting for transfers between devices, shards(): piece = lax.all_gather(grad_hidden, ('gx', 'gz'), axis=0, tiled=True)  144 us
    all_to_all x1, waiting for transfers between devices, shards(): lax.all_to_all(summed, 'gx', split_axis=0, concat_axis=1, tiled=True)  29.3 us
    all_to_all x1, starting transfers between devices, shards(): lax.all_to_all(summed, 'gx', split_axis=0, concat_axis=1, tiled=True)  19.8 us
    all_to_all x1, starting transfers between devices, shards(): lax.all_to_all(inputs, 'gx', split_axis=1, concat_axis=0, tiled=True)  12.5 us
  transfers between devices with their start and end apart: 3, of which 2 were waited for; matrix products, arithmetic and copies ran while one was open for 4% of the time, Pallas kernels for 0%

commit v1 on v0

v1 whole, which is shorter than its diff:
```python
import jax
import jax.numpy as jnp
from jax import lax
from jax.sharding import Mesh
from jax.sharding import PartitionSpec as P

RING = (0, 2, 4, 6, 7, 5, 3, 1)
PLACE = tuple(RING.index(k) for k in range(8))
F32 = jnp.float32
BF16 = jnp.bfloat16


def gelu_slope(value):
    scale = 0.7978845608028654
    tangent = jnp.tanh(scale * (value + 0.044715 * value * value * value))
    inner = scale * (1.0 + 3.0 * 0.044715 * value * value)
    return 0.5 * (1.0 + tangent) + 0.5 * value * (1.0 - tangent * tangent) * inner


def hop(value, step):
    return lax.ppermute(value, "gx", [(RING[q], RING[(q + step) % 8]) for q in range(8)])


def swap(value):
    return lax.ppermute(value, "core", [(0, 1), (1, 0)])


def shards(inputs, weight, grad_out, pre_act):
    core = lax.axis_index("core")
    place = jnp.asarray(PLACE, jnp.int32)[lax.axis_index("gx")]
    gh = (grad_out.astype(F32) * gelu_slope(pre_act.astype(F32))).astype(BF16)
    other_weight = swap(weight)

    part = lax.dynamic_slice(inputs, (lax.axis_index("x") * 64, 0), (64, 1536))
    part = part.reshape(2, 32, 8, 192).transpose(2, 0, 1, 3).reshape(512, 192)
    part = lax.all_to_all(part, ("gx", "core"), split_axis=0, concat_axis=0, tiled=True)
    cols = lax.all_gather(part.reshape(8, 2, 32, 192), "x", axis=0)
    cols = jnp.where(core == 0, cols, cols[:, :, ::-1])
    cols = jnp.stack([cols[:, k] for k in RING], 0)
    cols = lax.dynamic_slice_in_dim(jnp.concatenate([cols, cols], 0), (place + 4) % 8, 8, 0)
    cols = cols.transpose(0, 1, 3, 2, 4)

    up, down = [gh], [gh]
    for _ in range(3):
        up.append(hop(up[-1], 1))
        down.append(hop(down[-1], -1))
    last = jnp.concatenate([hop(up[3][:16], 1), hop(down[3][16:], -1)], 0)
    groups = [([4], gh[None])]
    groups += [([4 - s, 4 + s], jnp.stack([up[s], down[s]], 0)) for s in (1, 2, 3)]
    groups += [([0], last[None])]
    blocks = [None] * 8
    weight_sum = 0.0
    for places, value in groups:
        n = len(places)
        full = lax.all_gather(value, "y", axis=0)
        flat = full.reshape(128 * n, 3072)
        mine = jnp.stack([cols[p] for p in places], 1).reshape(128 * n, 384)
        weight_sum = weight_sum + lax.dot_general(
            mine, flat, (((0,), (0,)), ((), ())), preferred_element_type=F32
        )
        halves = [
            lax.dot_general(flat, w, (((1,), (1,)), ((), ())), preferred_element_type=F32)
            .astype(BF16)
            .reshape(4, n, 32, 192)
            for w in (weight, other_weight)
        ]
        for i, p in enumerate(places):
            blocks[p] = jnp.stack([h[:, i] for h in halves], 1)

    rows = jnp.stack(blocks, 0)
    rows = lax.dynamic_slice_in_dim(jnp.concatenate([rows, rows], 0), (12 - place) % 8, 8, 0)
    rows = jnp.where(core == 0, rows, rows[:, :, ::-1])
    rows = jnp.stack([rows[q] for q in PLACE], 1)
    rows = lax.all_to_all(rows, "x", split_axis=0, concat_axis=0, tiled=True)
    rows = jnp.sum(rows.astype(F32), 0).astype(BF16)
    rows = jnp.stack([rows, rows], 1).reshape(32, 32, 192)
    rows = lax.all_to_all(rows, ("gx", "zh", "core"), split_axis=0, concat_axis=0, tiled=True)
    rows = jnp.sum(rows.reshape(8, 2, 2, 32, 192).astype(F32), 1).astype(BF16)
    rows = rows.transpose(1, 2, 0, 3).reshape(64, 1536)
    grad_in = lax.all_gather(rows, "x", axis=0, tiled=True)

    grad_weight = (weight_sum[:192] + swap(weight_sum[192:])).astype(BF16)
    return grad_in, grad_weight


def solution(mesh):
    fine = Mesh(mesh.devices.reshape(8, 4, 2, 4, 2), ("gx", "x", "zh", "y", "core"))
    split = P(("gx", "y", "core"), ("x", "zh"))
    tokens = P("gx", ("y", "core"))
    rows = P(("y", "core", "gx"), ("x", "zh"))
    return jax.shard_map(
        shards,
        mesh=fine,
        in_specs=(tokens, rows, split, split),
        out_specs=(tokens, rows),
        check_vma=False,
    )
```

time: 526 us -> 310 us (0.59)
  the two profiles are of different devices: /device:TPU:16 before, /device:TPU:32 now
where the time goes in v1:
time: 310 us; the launch traced here: 305 us
  blocking collectives  98.5 us (32%)
  local copies, waits for them, and re-layouts  50.9 us (16%)
  starting transfers between devices  47.1 us (15%)
  matrix products  40 us (13%)
  other arithmetic  28.2 us (9%)
  waiting for transfers between devices  24.9 us (8%)
  between operations  15.7 us (5%)
    all_to_all x1, blocking collectives, shards(): lax.all_to_all(rows, ('gx', 'zh', 'core'), split_axis=0, concat_axis=0, t...  38.7 us
    ppermute x8, starting transfers between devices, hop(): lax.ppermute(value, 'gx', [(RING[q], RING[(q + step) % 8]) for q in range...  30.2 us
    all_gather x2, blocking collectives, shards(): full = lax.all_gather(value, 'y', axis=0)  29.8 us
    ppermute x8, waiting for transfers between devices, hop(): lax.ppermute(value, 'gx', [(RING[q], RING[(q + step) % 8]) for q in range...  24.9 us
    dot_general x5, matrix products, shards(): lax.dot_general(mine, flat, (((0,), (0,)), ((), ())), preferred_element_t...  20.5 us
    dot_general x10, matrix products, shards(): lax.dot_general(flat, w, (((1,), (1,)), ((), ())), preferred_element_type...  19.5 us
    all_gather x1, blocking collectives, shards(): cols = lax.all_gather(part.reshape(8, 2, 32, 192), 'x', axis=0)  15 us
    all_gather x1, blocking collectives, shards(): grad_in = lax.all_gather(rows, 'x', axis=0, tiled=True)  14.9 us
  transfers between devices with their start and end apart: 15, of which 6 were waited for; matrix products, arithmetic and copies ran while one was open for 30% of the time, Pallas kernels for 0%

profile of v1, /device:TPU:32, one launch (start us, length us, event | category | flops | bytes accessed | tf_op | source)
XLA Modules:
  0.0 305.3 jit_solution(5362394011430778921)
XLA Ops:
  8.6 5.2 %collective-permute-start.4 = (bf16[32,3072]{1,0:T(8,128)(2,1)S(1)}, bf16[32,3072]{1,0:T(8,128)(2,1)S(1)}, u32[]{:S(2)}, u32[]{:S(2)}) collective-permute-start(bf16[32,3072]{1,0:T(8,128)(2,1)S(1)} %fusion.7), channel_id=1, source_target_pairs={{0,64},{128,0},{256,128},{384,256},{448,384},{320,448},{192,320},{... | collective-permute-start | bytes 589832 | tf_op jit(solution)/shard_map/ppermute | solution.py:21
  13.8 4.1 %collective-permute-start = (bf16[32,3072]{1,0:T(8,128)(2,1)S(1)}, bf16[32,3072]{1,0:T(8,128)(2,1)S(1)}, u32[]{:S(2)}, u32[]{:S(2)}) collective-permute-start(bf16[32,3072]{1,0:T(8,128)(2,1)S(1)} %fusion.7), channel_id=1, source_target_pairs={{0,128},{128,256},{256,384},{384,448},{448,320},{320,192},{192,64}... | collective-permute-start | bytes 589832 | tf_op jit(solution)/shard_map/ppermute | solution.py:21
  17.9 2.5 collective-permute-done.4
  20.5 5.0 %collective-permute-done = bf16[32,3072]{1,0:T(8,128)(2,1)S(1)} collective-permute-done((bf16[32,3072]{1,0:T(8,128)(2,1)S(1)}, bf16[32,3072]{1,0:T(8,128)(2,1)S(1)}, u32[]{:S(2)}, u32[]{:S(2)}) %collective-permute-start) | collective-permute-done | bytes 196640 | tf_op jit(solution)/shard_map/ppermute | solution.py:21
  26.3 5.2 %collective-permute-start.5 = (bf16[32,3072]{1,0:T(8,128)(2,1)S(1)}, bf16[32,3072]{1,0:T(8,128)(2,1)S(1)}, u32[]{:S(2)}, u32[]{:S(2)}) collective-permute-start(bf16[32,3072]{1,0:T(8,128)(2,1)S(1)} %collective-permute-done.4), channel_id=1, source_target_pairs={{0,64},{128,0},{256,128},{384,256},{448,384},{320,448},{192,320},{... | collective-permute-start | bytes 589832 | tf_op jit(solution)/shard_map/ppermute | solution.py:21
  33.4 5.3 %collective-permute-done.5 = bf16[32,3072]{1,0:T(8,128)(2,1)S(1)} collective-permute-done((bf16[32,3072]{1,0:T(8,128)(2,1)S(1)}, bf16[32,3072]{1,0:T(8,128)(2,1)S(1)}, u32[]{:S(2)}, u32[]{:S(2)}) %collective-permute-start.5) | collective-permute-done | bytes 196640 | tf_op jit(solution)/shard_map/ppermute | solution.py:21
  38.8 2.2 collective-permute-done.1
  42.8 8.5 %all-to-all-start.2 = ((bf16[16,32,192]{2,1,0:T(8,128)(2,1)}), bf16[16,32,192]{2,1,0:T(8,128)(2,1)S(1)}, u32[]{:S(2)}, u32[]{:S(2)}) async-start(bf16[16,32,192]{2,1,0:T(8,128)(2,1)} %bitcast.41), calls=%async_computation.2 | async-start | bytes 524288 | tf_op jit(solution)/shard_map/all_to_all | solution.py:36
  55.4 16.0 %all-gather.4 = bf16[128,3072]{1,0:T(8,128)(2,1)S(1)} all-gather(bf16[32,3072]{1,0:T(8,128)(2,1)} %copy-done.8), channel_id=6, replica_groups=mesh['gx'=8,'x'=4,'zh'=2,'y'=4,'core'=2] {'y'}, dimensions={0}, use_global_device_ids=true | all-gather | bytes 983040 | tf_op jit(solution)/shard_map/all_gather | solution.py:55
  71.4 4.5 %collective-permute-start.6 = (bf16[32,3072]{1,0:T(8,128)(2,1)}, bf16[32,3072]{1,0:T(8,128)(2,1)}, u32[]{:S(2)}, u32[]{:S(2)}) collective-permute-start(bf16[32,3072]{1,0:T(8,128)(2,1)} %copy-done.23), channel_id=1, source_target_pairs={{0,64},{128,0},{256,128},{384,256},{448,384},{320,448},{192,320},{... | collective-permute-start | bytes 589832 | tf_op jit(solution)/shard_map/ppermute | solution.py:21
  79.1 4.2 %collective-permute-done.6 = bf16[32,3072]{1,0:T(8,128)(2,1)} collective-permute-done((bf16[32,3072]{1,0:T(8,128)(2,1)}, bf16[32,3072]{1,0:T(8,128)(2,1)}, u32[]{:S(2)}, u32[]{:S(2)}) %collective-permute-start.6) | collective-permute-done | bytes 196640 | tf_op jit(solution)/shard_map/ppermute | solution.py:21
  84.2 5.5 %collective-permute-start.7 = (bf16[16,3072]{1,0:T(8,128)(2,1)S(1)}, bf16[16,3072]{1,0:T(8,128)(2,1)}, u32[]{:S(2)}, u32[]{:S(2)}) collective-permute-start(bf16[16,3072]{1,0:T(8,128)(2,1)S(1)} %slice.161), channel_id=1, source_target_pairs={{0,64},{128,0},{256,128},{384,256},{448,384},{320,448},{192,320},{... | collective-permute-start | bytes 294920 | tf_op jit(solution)/shard_map/ppermute | solution.py:21
  95.0 5.6 %collective-permute-done.3 = bf16[16,3072]{1,0:T(8,128)(2,1)} collective-permute-done((bf16[16,3072]{1,0:T(8,128)(2,1)}, bf16[16,3072]{1,0:T(8,128)(2,1)}, u32[]{:S(2)}, u32[]{:S(2)}) %collective-permute-start.3) | collective-permute-done | bytes 98336 | tf_op jit(solution)/shard_map/ppermute | solution.py:21
  101.6 13.8 %all-gather = bf16[128,3072]{1,0:T(8,128)(2,1)S(1)} all-gather(bf16[32,3072]{1,0:T(8,128)(2,1)S(1)} %pad_maximum_fusion.7), channel_id=2, replica_groups=mesh['gx'=8,'x'=4,'zh'=2,'y'=4,'core'=2] {'y'}, dimensions={0}, use_global_device_ids=true | all-gather | bytes 983040 | tf_op jit(solution)/shard_map/all_gather | solution.py:55
  117.8 15.0 %all_gather.39 = bf16[4,8,2,32,192]{4,2,3,0,1:T(2,128)(2,1)} all-gather(bf16[1,8,2,32,192]{4,2,3,0,1:T(2,128)(2,1)S(1)} %copy.132), channel_id=1, replica_groups=mesh['gx'=8,'x'=4,'zh'=2,'y'=4,'core'=2] {'x'}, dimensions={0}, use_global_device_ids=true | all-gather | bytes 983040 | tf_op jit(solution)/shard_map/all_gather | solution.py:37
  132.8 10.2 %rev.7 = bf16[4,8,2,32,192]{4,2,3,0,1:T(2,128)(2,1)} reverse(bf16[4,8,2,32,192]{4,2,3,0,1:T(2,128)(2,1)} %all_gather.39), dimensions={2} | reverse | bytes 1572864 | tf_op jit(solution)/shard_map/rev | solution.py:38
  153.9 2.6 pad_maximum_fusion.4
  162.2 4.2 %fusion.35 = f32[384,3072]{1,0:T(8,128)} fusion(bf16[128,384]{1,0:T(8,128)(2,1)} %reshape_stack_squeeze.6, bf16[128,3072]{1,0:T(8,128)(2,1)} %copy-done.6), kind=kOutput, calls=%fused_computation.125 | convolution fusion | flops 301989888 | bytes 5603328 | tf_op jit(solution)/shard_map/dot_general | solution.py:58
  169.1 2.2 convolution_convert_fusion.8
  174.4 2.7 convolution_convert_fusion.1
  178.7 2.7 convolution_convert_fusion
  184.7 4.5 %fusion.36 = f32[384,3072]{1,0:T(8,128)} fusion(bf16[256,384]{1,0:T(8,128)(2,1)} %reshape.82, bf16[256,3072]{1,0:T(8,128)(2,1)} %bitcast.231), kind=kOutput, calls=%fused_computation.126 | convolution fusion | flops 603979776 | bytes 6488064 | tf_op jit(solution)/shard_map/dot_general | solution.py:58
  189.2 2.7 convolution_convert_fusion.3
  193.6 2.7 convolution_convert_fusion.2
  199.6 4.4 %fusion.37 = f32[384,3072]{1,0:T(8,128)} fusion(bf16[256,384]{1,0:T(8,128)(2,1)S(1)} %reshape.83, bf16[256,3072]{1,0:T(8,128)(2,1)} %bitcast.234), kind=kOutput, calls=%fused_computation.127 | convolution fusion | flops 603979776 | bytes 6488064 | tf_op jit(solution)/shard_map/dot_general | solution.py:58
  204.1 2.1 convolution_convert_fusion.5
  206.4 2.2 convolution_convert_fusion.4
  221.6 4.3 %all-to-all-start = ((bf16[4,8,2,32,192]{4,3,2,1,0:T(8,128)(2,1)}), bf16[4,8,2,32,192]{4,3,2,1,0:T(8,128)(2,1)}, u32[]{:S(2)}, u32[]{:S(2)}) async-start(bf16[4,8,2,32,192]{4,3,2,1,0:T(8,128)(2,1)} %copy.129), calls=%async_computation | async-start | bytes 2097152 | tf_op jit(solution)/shard_map/all_to_all | solution.py:74
  227.0 6.6 %add_add_fusion = f32[384,3072]{1,0:T(8,128)S(1)} fusion(f32[384,3072]{1,0:T(8,128)S(1)} %fusion.38, f32[384,3072]{1,0:T(8,128)} %fusion.37, f32[384,3072]{1,0:T(8,128)} %fusion.35, f32[384,3072]{1,0:T(8,128)} %fusion.36, bf16[128,384]{1,0:T(8,128)(2,1)S(1)} %copy-done.21, bf16[128,3072]{1,0:T(8,128)(2,1)S(1)} %copy-done.5), kind=kOutput, calls=%fused_computation | convolution fusion | flops 306708480 | bytes 24477696 | tf_op jit(solution)/shard_map/dot_general | solution.py:58
  240.1 38.7 %all_to_all.19 = bf16[32,32,192]{2,1,0:T(8,128)(2,1)S(1)} all-to-all(bf16[32,32,192]{2,1,0:T(8,128)(2,1)S(1)} %bitcast.257), channel_id=1, replica_groups=mesh['gx'=8,'x'=4,'zh'=2,'y'=4,'core'=2] {'gx','zh','core'}, dimensions={0} | all-to-all | bytes 786432 | tf_op jit(solution)/shard_map/all_to_all | solution.py:77
  279.3 14.9 %all_gather.38 = bf16[256,1536]{1,0:T(8,128)(2,1)S(1)} all-gather(bf16[64,1536]{1,0:T(8,128)(2,1)S(1)} %reshape.80), channel_id=1, replica_groups=mesh['gx'=8,'x'=4,'zh'=2,'y'=4,'core'=2] {'x'}, dimensions={0}, use_global_device_ids=true | all-gather | bytes 983040 | tf_op jit(solution)/shard_map/all_gather | solution.py:80
  294.2 3.7 %fusion = bf16[192,3072]{1,0:T(8,128)(2,1)} fusion(f32[192,3072]{1,0:T(8,128)} %collective-permute-done.9, f32[384,3072]{1,0:T(8,128)} %copy-done.2), kind=kLoop, calls=%fused_computation.2 | loop fusion | flops 1179648 | bytes 5898240 | tf_op jit(solution)/shard_map/convert_element_type | solution.py:82
  (161 shorter events, 75.4 us)
Async XLA Ops:
  7.2 34.7 %copy-start = (bf16[256,1536]{1,0:T(8,128)(2,1)S(1)}, bf16[256,1536]{1,0:T(8,128)(2,1)}, u32[]{:S(2)}) copy-start(bf16[256,1536]{1,0:T(8,128)(2,1)} %param.5) | copy-start | bytes 2359300
  7.2 167.2 %all-gather.13.cloned.1.call-start = ((), (), s32[]{:S(2)}) async-start(), calls=%async_computation.5 | async-start | bytes 1966080 | tf_op jit(solution)/shard_map/all_gather | solution.py:55
  8.6 16.9 %copy-start.8 = (bf16[32,3072]{1,0:T(8,128)(2,1)}, bf16[32,3072]{1,0:T(8,128)(2,1)S(1)}, u32[]{:S(2)}) copy-start(bf16[32,3072]{1,0:T(8,128)(2,1)S(1)} %fusion.7) | copy-start | bytes 589828
  8.6 11.9 %collective-permute-start.4 = (bf16[32,3072]{1,0:T(8,128)(2,1)S(1)}, bf16[32,3072]{1,0:T(8,128)(2,1)S(1)}, u32[]{:S(2)}, u32[]{:S(2)}) collective-permute-start(bf16[32,3072]{1,0:T(8,128)(2,1)S(1)} %fusion.7), channel_id=1, source_target_pairs={{0,64},{128,0},{256,128},{384,256},{448,384},{320,448},{192,320},{... | collective-permute-start | bytes 589832 | tf_op jit(solution)/shard_map/ppermute | solution.py:21
  13.8 11.7 %collective-permute-start = (bf16[32,3072]{1,0:T(8,128)(2,1)S(1)}, bf16[32,3072]{1,0:T(8,128)(2,1)S(1)}, u32[]{:S(2)}, u32[]{:S(2)}) collective-permute-start(bf16[32,3072]{1,0:T(8,128)(2,1)S(1)} %fusion.7), channel_id=1, source_target_pairs={{0,128},{128,256},{256,384},{384,448},{448,320},{320,192},{192,64}... | collective-permute-start | bytes 589832 | tf_op jit(solution)/shard_map/ppermute | solution.py:21
  25.5 26.0 %copy-start.1 = (bf16[192,3072]{1,0:T(8,128)(2,1)S(1)}, bf16[192,3072]{1,0:T(8,128)(2,1)}, u32[]{:S(2)}) copy-start(bf16[192,3072]{1,0:T(8,128)(2,1)} %param.6) | copy-start | bytes 3538948
  25.5 28.1 %copy-start.24 = (s32[8]{0:T(128)S(1)}, s32[8]{0:T(128)}, u32[]{:S(2)}) copy-start(s32[8]{0:T(128)} %constant.62.clone) | copy-start | bytes 100
  26.3 163.0 %all-gather.11.cloned.1.call-start = ((), (), s32[]{:S(2)}) async-start(), calls=%async_computation.4 | async-start | bytes 1966080 | tf_op jit(solution)/shard_map/all_gather | solution.py:55
  26.3 12.4 %collective-permute-start.5 = (bf16[32,3072]{1,0:T(8,128)(2,1)S(1)}, bf16[32,3072]{1,0:T(8,128)(2,1)S(1)}, u32[]{:S(2)}, u32[]{:S(2)}) collective-permute-start(bf16[32,3072]{1,0:T(8,128)(2,1)S(1)} %collective-permute-done.4), channel_id=1, source_target_pairs={{0,64},{128,0},{256,128},{384,256},{448,384},{320,448},{192,320},{... | collective-permute-start | bytes 589832 | tf_op jit(solution)/shard_map/ppermute | solution.py:21
  31.5 9.5 %collective-permute-start.1 = (bf16[32,3072]{1,0:T(8,128)(2,1)S(1)}, bf16[32,3072]{1,0:T(8,128)(2,1)S(1)}, u32[]{:S(2)}, u32[]{:S(2)}) collective-permute-start(bf16[32,3072]{1,0:T(8,128)(2,1)S(1)} %collective-permute-done), channel_id=1, source_target_pairs={{0,128},{128,256},{256,384},{384,448},{448,320},{320,192},{192,64}... | collective-permute-start | bytes 589832 | tf_op jit(solution)/shard_map/ppermute | solution.py:21
  42.8 74.7 %all-to-all-start.2 = ((bf16[16,32,192]{2,1,0:T(8,128)(2,1)}), bf16[16,32,192]{2,1,0:T(8,128)(2,1)S(1)}, u32[]{:S(2)}, u32[]{:S(2)}) async-start(bf16[16,32,192]{2,1,0:T(8,128)(2,1)} %bitcast.41), calls=%async_computation.2 | async-start | bytes 524288 | tf_op jit(solution)/shard_map/all_to_all | solution.py:36
  51.4 152.7 %all-gather.9.cloned.1.call-start = ((), (), s32[]{:S(2)}) async-start(), calls=%async_computation.3 | async-start | bytes 1966080 | tf_op jit(solution)/shard_map/all_gather | solution.py:55
  51.4 115.0 %collective-permute-start.8 = (bf16[192,3072]{1,0:T(8,128)(2,1)S(1)}, bf16[192,3072]{1,0:T(8,128)(2,1)S(1)}, u32[]{:S(2)}, u32[]{:S(2)}) collective-permute-start(bf16[192,3072]{1,0:T(8,128)(2,1)S(1)} %copy-done.1), channel_id=1, source_target_pairs={{0,1},{1,0},{2,3},{3,2},{4,5},{5,4},{6,7},{7,6},{8,9},{9,8},{10,11... | collective-permute-start | bytes 3538952 | tf_op jit(solution)/shard_map/ppermute | solution.py:25
  71.4 6.5 %copy-start.6 = (bf16[128,3072]{1,0:T(8,128)(2,1)}, bf16[128,3072]{1,0:T(8,128)(2,1)S(1)}, u32[]{:S(2)}) copy-start(bf16[128,3072]{1,0:T(8,128)(2,1)S(1)} %all-gather.4) | copy-start | bytes 2359300
  71.4 11.9 %collective-permute-start.6 = (bf16[32,3072]{1,0:T(8,128)(2,1)}, bf16[32,3072]{1,0:T(8,128)(2,1)}, u32[]{:S(2)}, u32[]{:S(2)}) collective-permute-start(bf16[32,3072]{1,0:T(8,128)(2,1)} %copy-done.23), channel_id=1, source_target_pairs={{0,64},{128,0},{256,128},{384,256},{448,384},{320,448},{192,320},{... | collective-permute-start | bytes 589832 | tf_op jit(solution)/shard_map/ppermute | solution.py:21
  75.9 13.8 %collective-permute-start.2 = (bf16[32,3072]{1,0:T(8,128)(2,1)}, bf16[32,3072]{1,0:T(8,128)(2,1)}, u32[]{:S(2)}, u32[]{:S(2)}) collective-permute-start(bf16[32,3072]{1,0:T(8,128)(2,1)} %copy-done.22), channel_id=1, source_target_pairs={{0,128},{128,256},{256,384},{384,448},{448,320},{320,192},{192,64}... | collective-permute-start | bytes 589832 | tf_op jit(solution)/shard_map/ppermute | solution.py:21
  84.2 10.8 %collective-permute-start.7 = (bf16[16,3072]{1,0:T(8,128)(2,1)S(1)}, bf16[16,3072]{1,0:T(8,128)(2,1)}, u32[]{:S(2)}, u32[]{:S(2)}) collective-permute-start(bf16[16,3072]{1,0:T(8,128)(2,1)S(1)} %slice.161), channel_id=1, source_target_pairs={{0,64},{128,0},{256,128},{384,256},{448,384},{320,448},{192,320},{... | collective-permute-start | bytes 294920 | tf_op jit(solution)/shard_map/ppermute | solution.py:21
  91.2 9.4 %collective-permute-start.3 = (bf16[16,3072]{1,0:T(8,128)(2,1)}, bf16[16,3072]{1,0:T(8,128)(2,1)}, u32[]{:S(2)}, u32[]{:S(2)}) collective-permute-start(bf16[16,3072]{1,0:T(8,128)(2,1)} %slice.160), channel_id=1, source_target_pairs={{0,128},{128,256},{256,384},{384,448},{448,320},{320,192},{192,64}... | collective-permute-start | bytes 294920 | tf_op jit(solution)/shard_map/ppermute | solution.py:21
  162.2 4.2 %copy-start.7 = (bf16[128,3072]{1,0:T(8,128)(2,1)S(1)}, bf16[128,3072]{1,0:T(8,128)(2,1)}, u32[]{:S(2)}) copy-start(bf16[128,3072]{1,0:T(8,128)(2,1)} %copy-done.6) | copy-start | bytes 2359300
  206.3 3.8 %copy-start.15 = (bf16[4,1,32,192]{3,2,0,1:T(8,128)(2,1)S(1)}, bf16[4,1,32,192]{3,2,0,1:T(8,128)(2,1)}, u32[]{:S(2)}) copy-start(bf16[4,1,32,192]{3,2,0,1:T(8,128)(2,1)} %get-tuple-element.21) | copy-start | bytes 147460
  206.3 3.8 %copy-start.16 = (bf16[4,1,32,192]{3,2,0,1:T(8,128)(2,1)S(1)}, bf16[4,1,32,192]{3,2,0,1:T(8,128)(2,1)}, u32[]{:S(2)}) copy-start(bf16[4,1,32,192]{3,2,0,1:T(8,128)(2,1)} %get-tuple-element.26) | copy-start | bytes 147460
  206.3 4.5 %copy-start.9 = (bf16[128,192]{1,0:T(8,128)(2,1)S(1)}, bf16[128,192]{1,0:T(8,128)(2,1)}, u32[]{:S(2)}) copy-start(bf16[128,192]{1,0:T(8,128)(2,1)} %copy.121) | copy-start | bytes 147460
  206.3 4.4 %copy-start.11 = (bf16[128,192]{1,0:T(8,128)(2,1)S(1)}, bf16[128,192]{1,0:T(8,128)(2,1)}, u32[]{:S(2)}) copy-start(bf16[128,192]{1,0:T(8,128)(2,1)} %copy.122) | copy-start | bytes 147460
  206.3 5.1 %copy-start.13 = (bf16[4,1,32,192]{3,2,0,1:T(8,128)(2,1)S(1)}, bf16[4,1,32,192]{3,2,0,1:T(8,128)(2,1)}, u32[]{:S(2)}) copy-start(bf16[4,1,32,192]{3,2,0,1:T(8,128)(2,1)} %get-tuple-element.20) | copy-start | bytes 147460
  206.3 5.1 %copy-start.14 = (bf16[4,1,32,192]{3,2,0,1:T(8,128)(2,1)S(1)}, bf16[4,1,32,192]{3,2,0,1:T(8,128)(2,1)}, u32[]{:S(2)}) copy-start(bf16[4,1,32,192]{3,2,0,1:T(8,128)(2,1)} %get-tuple-element.27) | copy-start | bytes 147460
  206.3 5.8 %copy-start.17 = (bf16[4,1,32,192]{3,2,0,1:T(8,128)(2,1)S(1)}, bf16[4,1,32,192]{3,2,0,1:T(8,128)(2,1)}, u32[]{:S(2)}) copy-start(bf16[4,1,32,192]{3,2,0,1:T(8,128)(2,1)} %get-tuple-element.16) | copy-start | bytes 147460
  206.4 5.8 %copy-start.18 = (bf16[4,1,32,192]{3,2,0,1:T(8,128)(2,1)S(1)}, bf16[4,1,32,192]{3,2,0,1:T(8,128)(2,1)}, u32[]{:S(2)}) copy-start(bf16[4,1,32,192]{3,2,0,1:T(8,128)(2,1)} %get-tuple-element.25) | copy-start | bytes 147460
  206.4 7.1 %copy-start.10 = (bf16[128,192]{1,0:T(8,128)(2,1)S(1)}, bf16[128,192]{1,0:T(8,128)(2,1)}, u32[]{:S(2)}) copy-start(bf16[128,192]{1,0:T(8,128)(2,1)} %copy.107) | copy-start | bytes 147460
  206.4 7.1 %copy-start.12 = (bf16[128,192]{1,0:T(8,128)(2,1)S(1)}, bf16[128,192]{1,0:T(8,128)(2,1)}, u32[]{:S(2)}) copy-start(bf16[128,192]{1,0:T(8,128)(2,1)} %copy.108) | copy-start | bytes 147460
  220.5 5.3 %copy-start.3 = (bf16[8,32,3072]{2,1,0:T(8,128)(2,1)S(1)}, bf16[8,32,3072]{2,1,0:T(8,128)(2,1)}, u32[]{:S(2)}) copy-start(bf16[8,32,3072]{2,1,0:T(8,128)(2,1)} %all-gather.9.cloned.1.call-done) | copy-start | bytes 4718596
  221.6 16.9 %all-to-all-start = ((bf16[4,8,2,32,192]{4,3,2,1,0:T(8,128)(2,1)}), bf16[4,8,2,32,192]{4,3,2,1,0:T(8,128)(2,1)}, u32[]{:S(2)}, u32[]{:S(2)}) async-start(bf16[4,8,2,32,192]{4,3,2,1,0:T(8,128)(2,1)} %copy.129), calls=%async_computation | async-start | bytes 2097152 | tf_op jit(solution)/shard_map/all_to_all | solution.py:74
  236.6 57.6 %collective-permute-start.9 = (f32[192,3072]{1,0:T(8,128)}, f32[192,3072]{1,0:T(8,128)}, u32[]{:S(2)}, u32[]{:S(2)}) collective-permute-start(f32[192,3072]{1,0:T(8,128)} %slice.199), channel_id=1, source_target_pairs={{0,1},{1,0},{2,3},{3,2},{4,5},{5,4},{6,7},{7,6},{8,9},{9,8},{10,11... | collective-permute-start | bytes 7077896 | tf_op jit(solution)/shard_map/ppermute | solution.py:25
  (8 other events, 16.5 us)
Sparse Core Ops, SparseCore 0:
  26.4 38.1 all-gather.12
  66.7 39.2 all-gather.10
  108.1 37.3 all-gather.8

commit v2 on v0

v2 whole, which is shorter than its diff:
```python
import jax
import jax.numpy as jnp
from jax import lax
from jax.experimental import pallas as pl
from jax.experimental.pallas import tpu as pltpu
from jax.sharding import Mesh
from jax.sharding import PartitionSpec as P

RING = (0, 2, 4, 6, 7, 5, 3, 1)
PLACE = tuple(RING.index(k) for k in range(8))
STEPS = (0, -1, 1, -2, 2, -3, 3, 4)
F32 = jnp.float32
BF16 = jnp.bfloat16
SMEM = pl.BlockSpec(memory_space=pltpu.SMEM)
VMEM = pl.BlockSpec(memory_space=pltpu.VMEM)
LIMIT = pltpu.CompilerParams(vmem_limit_bytes=48 * 1024 * 1024)


def gelu_slope(value):
    scale = 0.7978845608028654
    tangent = jnp.tanh(scale * (value + 0.044715 * value * value * value))
    inner = scale * (1.0 + 3.0 * 0.044715 * value * value)
    return 0.5 * (1.0 + tangent) + 0.5 * value * (1.0 - tangent * tangent) * inner


def hop(value, step):
    return lax.ppermute(value, "gx", [(RING[q], RING[(q + step) % 8]) for q in range(8)])


def swap(value, axis):
    return lax.ppermute(value, axis, [(0, 1), (1, 0)])


def across(value):
    return lax.ppermute(value, ("yp", "yl"), [(k, 3 - k) for k in range(4)])


def product_kernel(owner, dest, *refs):
    pieces, weights, (rows, whole) = refs[:12], refs[12:16], refs[16:]
    at = 0
    for piece in pieces:
        whole[at : at + piece.shape[0]] = piece[...]
        at += piece.shape[0]
    for j, weight in enumerate(weights):
        block = lax.dot_general(
            whole[...], weight[...], (((1,), (1,)), ((), ())), preferred_element_type=F32
        ).astype(BF16)
        for side in range(2):
            for slot in range(8):
                for half in range(2):
                    first = side * 256 + slot * 32 + half * 16
                    rows[side * 2 + half, dest[j], owner[slot]] = block[first : first + 16]


def weight_kernel(owner, dest, cols, whole, keep, send, turned):
    @pl.when(pl.program_id(0) == 0)
    def _():
        for j in range(4):
            parts = [
                cols[side * 2 + half, owner[slot], dest[j]]
                for side in range(2)
                for slot in range(8)
                for half in range(2)
            ]
            turned[j * 192 : (j + 1) * 192] = jnp.concatenate(parts, 0).T

    total = jnp.dot(turned[...], whole[...], preferred_element_type=F32)
    for j in range(2):
        keep[j] = total[j * 192 : (j + 1) * 192]
        send[j] = total[384 + j * 192 : 384 + (j + 1) * 192]


def add_kernel(parts, out):
    for k in range(8):
        for j in range(4):
            total = parts[0, j, k].astype(F32)
            for i in range(1, 4):
                total = total + parts[i, j, k].astype(F32)
            total = total.astype(BF16)
            out[k, 0, j] = total
            out[k, 1, j] = total


def pair_kernel(parts, out):
    sums = [parts[k, 0].astype(F32) + parts[k, 1].astype(F32) for k in range(8)]
    out[...] = jnp.concatenate(sums, 1).astype(BF16)


def place_kernel(which, parts, out):
    mine = which[0]
    for p in range(2):
        side = jnp.where(mine == p, 0, 1)
        for s in range(2):
            source = jnp.where(mine == p, s, 1 - s)
            for c in range(2):
                for half in range(2):
                    first = p * 128 + s * 64 + c * 32 + half * 16
                    out[first : first + 16] = parts[side * 2 + half, source * 2 + c]


def shards(inputs, weight, grad_out, pre_act):
    x, yp, yl, core = (lax.axis_index(a) for a in ("x", "yp", "yl", "core"))
    place = jnp.asarray(PLACE, jnp.int32)[lax.axis_index("gx")]
    owner = jnp.asarray(RING, jnp.int32)[(place + jnp.asarray(STEPS, jnp.int32)) % 8]
    dest = jnp.stack([a * 2 + b for b in (core, 1 - core) for a in (yl, 1 - yl)]).astype(jnp.int32)

    gh = (grad_out.astype(F32) * gelu_slope(pre_act.astype(F32))).astype(BF16)

    beside = swap(weight, "yl")
    weights = (weight, beside, swap(weight, "core"), swap(beside, "core"))

    up, down = [gh], [gh]
    for _ in range(3):
        up.append(hop(up[-1], 1))
        down.append(hop(down[-1], -1))
    last = [hop(up[3][:16], 1), hop(down[3][16:], -1)]
    own = [gh, up[1], down[1], up[2], down[2], up[3], down[3], *last]
    far = [across(jnp.concatenate(v, 0)) for v in (own[:5], own[5:7], last)]

    part = lax.dynamic_slice(inputs, (jnp.where(x < 2, yp, 1 - yp) * 128, 0), (128, 1536))
    part = part.reshape(2, 2, 2, 16, 8, 192)
    part = jnp.where(x % 2 == 0, part[:, :, 0], part[:, :, 1])
    part = jnp.where(x < 2, part, part[::-1])
    part = part.transpose(3, 0, 1, 2, 4).reshape(32, 16, 192)
    part = lax.all_to_all(part, ("gx", "yl", "core"), split_axis=0, concat_axis=0, tiled=True)
    cols = lax.all_gather(part.reshape(8, 4, 16, 192), "x", axis=0)

    rows, whole = pl.pallas_call(
        product_kernel,
        out_shape=(
            jax.ShapeDtypeStruct((4, 4, 8, 16, 192), BF16),
            jax.ShapeDtypeStruct((512, 3072), BF16),
        ),
        in_specs=[SMEM, SMEM] + [VMEM] * 16,
        out_specs=(VMEM, VMEM),
        compiler_params=LIMIT,
        cost_estimate=pl.CostEstimate(
            flops=2 * 512 * 3072 * 768, bytes_accessed=12 << 20, transcendentals=0
        ),
        name="products",
    )(owner, dest, *own, *far, *weights)

    rows = lax.all_to_all(
        rows.reshape(16, 8, 16, 192), ("x", "yl", "core"), split_axis=0, concat_axis=0, tiled=True
    )
    rows = pl.pallas_call(
        add_kernel,
        out_shape=jax.ShapeDtypeStruct((8, 2, 4, 16, 192), BF16),
        in_specs=[VMEM],
        out_specs=VMEM,
        compiler_params=LIMIT,
        name="sum_x",
    )(rows.reshape(4, 4, 8, 16, 192))
    rows = lax.all_to_all(
        rows.reshape(16, 64, 192), ("gx", "zh"), split_axis=0, concat_axis=0, tiled=True
    )
    rows = pl.pallas_call(
        pair_kernel,
        out_shape=jax.ShapeDtypeStruct((64, 1536), BF16),
        in_specs=[VMEM],
        out_specs=VMEM,
        compiler_params=LIMIT,
        name="sum_z",
    )(rows.reshape(8, 2, 64, 192))
    rows = lax.all_gather(rows, "x", axis=0)
    grad_in = pl.pallas_call(
        place_kernel,
        out_shape=jax.ShapeDtypeStruct((256, 1536), BF16),
        in_specs=[SMEM, VMEM],
        out_specs=VMEM,
        compiler_params=LIMIT,
        name="place",
    )(yp.astype(jnp.int32)[None], rows.reshape(4, 4, 16, 1536))

    keep, send = pl.pallas_call(
        weight_kernel,
        grid=(6,),
        out_shape=(jax.ShapeDtypeStruct((2, 192, 3072), F32),) * 2,
        in_specs=[
            SMEM,
            SMEM,
            pl.BlockSpec((4, 8, 4, 16, 192), lambda i: (0, 0, 0, 0, 0)),
            pl.BlockSpec((512, 512), lambda i: (0, i)),
        ],
        out_specs=(pl.BlockSpec((2, 192, 512), lambda i: (0, 0, i)),) * 2,
        scratch_shapes=[pltpu.VMEM((768, 512), BF16)],
        compiler_params=LIMIT,
        cost_estimate=pl.CostEstimate(
            flops=2 * 512 * 3072 * 768, bytes_accessed=14 << 20, transcendentals=0
        ),
        name="weight_sums",
    )(owner, dest, cols, whole)
    met = swap(send, "core")
    passed = swap((keep[1] + met[1]).astype(BF16), "yl")
    grad_weight = (keep[0] + met[0] + passed.astype(F32)).astype(BF16)
    return grad_in, grad_weight


def solution(mesh):
    names = ("gx", "x", "zh", "yp", "yl", "core")
    fine = Mesh(mesh.devices.reshape(8, 4, 2, 2, 2, 2), names)
    split = P(("gx", "yp", "yl", "core"), ("x", "zh"))
    tokens = P("gx", ("yp", "yl", "core"))
    rows = P(("yp", "yl", "core", "gx"), ("x", "zh"))
    return jax.shard_map(
        shards,
        mesh=fine,
        in_specs=(tokens, rows, split, split),
        out_specs=(tokens, rows),
        check_vma=False,
    )
```

time: 526 us -> 204 us (0.39)
  the two profiles are of different devices: /device:TPU:16 before, /device:TPU:56 now
where the time goes in v2:
time: 204 us; the launch traced here: 203 us
  starting transfers between devices  81.1 us (40%)
  blocking collectives  48.8 us (24%)
  waiting for transfers between devices  36.7 us (18%)
  Pallas kernels  16.2 us (8%)
  other arithmetic  11.9 us (6%)
  local copies, waits for them, and re-layouts  7.13 us (3%)
    ppermute x8, starting transfers between devices, hop(): lax.ppermute(value, 'gx', [(RING[q], RING[(q + step) % 8]) for q in range...  31.3 us
    all_to_all x1, waiting for transfers between devices, shards(): lax.all_to_all(rows.reshape(16, 64, 192), ('gx', 'zh'), split_axis=0, con...  25.3 us
    all_to_all x1, blocking collectives, shards(): lax.all_to_all(rows.reshape(16, 8, 16, 192), ('x', 'yl', 'core'), split_a...  20.6 us
    all_gather x1, blocking collectives, shards(): cols = lax.all_gather(part.reshape(8, 4, 16, 192), 'x', axis=0)  14.8 us
    all_to_all x1, starting transfers between devices, shards(): lax.all_to_all(part, ('gx', 'yl', 'core'), split_axis=0, concat_axis=0, t...  13.5 us
    all_gather x1, blocking collectives, shards(): rows = lax.all_gather(rows, 'x', axis=0)  13.3 us
    all_to_all x1, starting transfers between devices, shards(): lax.all_to_all(rows.reshape(16, 64, 192), ('gx', 'zh'), split_axis=0, con...  13.1 us
    ppermute x5, starting transfers between devices, swap(): return lax.ppermute(value, axis, [(0, 1), (1, 0)])  11.9 us
  transfers between devices with their start and end apart: 18, of which 4 were waited for; matrix products, arithmetic and copies ran while one was open for 6% of the time, Pallas kernels for 1%

profile of v2, /device:TPU:56, one launch (start us, length us, event | category | flops | bytes accessed | tf_op | source)
XLA Modules:
  0.0 202.7 jit_solution(7155923436480033448)
XLA Ops:
  0.7 2.0 %constant_dynamic-update-slice_fusion.4 = (bf16[160,3072]{1,0:T(8,128)(2,1)}, bf16[32,3072]{1,0:T(8,128)(2,1)S(1)}) fusion(bf16[32,3072]{1,0:T(8,128)(2,1)} %param.10, bf16[32,3072]{1,0:T(8,128)(2,1)} %param.9), kind=kLoop, calls=%fused_computation.34 | loop fusion | flops 2064383 | bytes 786432
  2.7 5.2 %collective-permute-start.1 = (bf16[32,3072]{1,0:T(8,128)(2,1)S(1)}, bf16[32,3072]{1,0:T(8,128)(2,1)S(1)}, u32[]{:S(2)}, u32[]{:S(2)}) collective-permute-start(bf16[32,3072]{1,0:T(8,128)(2,1)S(1)} %get-tuple-element.11.refs_0_), channel_id=1, source_target_pairs={{0,64},{128,0},{256,128},{384,256},{448,384},{320,448},{192,320},{... | collective-permute-start | bytes 589832 | tf_op jit(solution)/shard_map/ppermute | solution.py:27
  7.9 1.9 collective-permute-start
  9.8 2.7 %collective-permute-start.11 = (bf16[192,3072]{1,0:T(8,128)(2,1)}, bf16[192,3072]{1,0:T(8,128)(2,1)}, u32[]{:S(2)}, u32[]{:S(2)}) collective-permute-start(bf16[192,3072]{1,0:T(8,128)(2,1)} %refs_12_.1), channel_id=1, source_target_pairs={{0,2},{2,0},{1,3},{3,1},{4,6},{6,4},{5,7},{7,5},{8,10},{10,8},{9,1... | collective-permute-start | bytes 3538952 | tf_op jit(solution)/shard_map/ppermute | solution.py:31
  12.5 1.9 collective-permute-start.12
  15.8 13.5 %all-to-all-start.2 = ((bf16[32,16,192]{2,1,0:T(8,128)(2,1)}), bf16[32,16,192]{2,1,0:T(8,128)(2,1)}, u32[]{:S(2)}, u32[]{:S(2)}) async-start(bf16[32,16,192]{2,1,0:T(8,128)(2,1)} %bitcast.13), calls=%async_computation.2 | async-start | bytes 524288 | tf_op jit(solution)/shard_map/all_to_all | solution.py:125
  30.6 4.3 %collective-permute-start.3 = (bf16[32,3072]{1,0:T(8,128)(2,1)S(1)}, bf16[32,3072]{1,0:T(8,128)(2,1)S(1)}, u32[]{:S(2)}, u32[]{:S(2)}) collective-permute-start(bf16[32,3072]{1,0:T(8,128)(2,1)S(1)} %collective-permute-done.1.refs_2_), channel_id=1, source_target_pairs={{0,64},{128,0},{256,128},{384,256},{448,384},{320,448},{192,320},{... | collective-permute-start | bytes 589832 | tf_op jit(solution)/shard_map/ppermute | solution.py:27
  34.8 1.9 collective-permute-start.2
  38.2 8.6 %collective-permute-done.3.refs_4_ = bf16[32,3072]{1,0:T(8,128)(2,1)S(1)} collective-permute-done((bf16[32,3072]{1,0:T(8,128)(2,1)S(1)}, bf16[32,3072]{1,0:T(8,128)(2,1)S(1)}, u32[]{:S(2)}, u32[]{:S(2)}) %collective-permute-start.3) | collective-permute-done | bytes 196640 | tf_op jit(solution)/shard_map/ppermute | solution.py:27
  46.7 7.1 %collective-permute-start.5 = (bf16[32,3072]{1,0:T(8,128)(2,1)S(1)}, bf16[32,3072]{1,0:T(8,128)(2,1)S(1)}, u32[]{:S(2)}, u32[]{:S(2)}) collective-permute-start(bf16[32,3072]{1,0:T(8,128)(2,1)S(1)} %collective-permute-done.3.refs_4_), channel_id=1, source_target_pairs={{0,64},{128,0},{256,128},{384,256},{448,384},{320,448},{192,320},{... | collective-permute-start | bytes 589832 | tf_op jit(solution)/shard_map/ppermute | solution.py:27
  53.8 1.9 collective-permute-start.4
  56.4 1.9 collective-permute-start.13
  59.1 1.9 collective-permute-start.8
  61.7 7.1 %collective-permute-start.7 = (bf16[16,3072]{1,0:T(8,128)(2,1)S(1)}, bf16[16,3072]{1,0:T(8,128)(2,1)S(1)}, u32[]{:S(2)}, u32[]{:S(2)}) collective-permute-start(bf16[16,3072]{1,0:T(8,128)(2,1)S(1)} %slice.35), channel_id=1, source_target_pairs={{0,64},{128,0},{256,128},{384,256},{448,384},{320,448},{192,320},{... | collective-permute-start | bytes 294920 | tf_op jit(solution)/shard_map/ppermute | solution.py:27
  68.9 1.9 collective-permute-start.6
  71.6 4.5 %collective-permute-start.9 = (bf16[64,3072]{1,0:T(8,128)(2,1)}, bf16[64,3072]{1,0:T(8,128)(2,1)}, u32[]{:S(2)}, u32[]{:S(2)}) collective-permute-start(bf16[64,3072]{1,0:T(8,128)(2,1)} %pad_maximum_fusion), channel_id=1, source_target_pairs={{0,6},{2,4},{4,2},{6,0},{1,7},{3,5},{5,3},{7,1},{8,14},{10,12},{12... | collective-permute-start | bytes 1179656 | tf_op jit(solution)/shard_map/ppermute | solution.py:35
  76.1 2.5 %collective-permute-done.6.refs_7_ = bf16[16,3072]{1,0:T(8,128)(2,1)S(1)} collective-permute-done((bf16[16,3072]{1,0:T(8,128)(2,1)S(1)}, bf16[16,3072]{1,0:T(8,128)(2,1)S(1)}, u32[]{:S(2)}, u32[]{:S(2)}) %collective-permute-start.6) | collective-permute-done | bytes 98336 | tf_op jit(solution)/shard_map/ppermute | solution.py:27
  79.3 4.8 %collective-permute-start.10 = (bf16[32,3072]{1,0:T(8,128)(2,1)}, bf16[32,3072]{1,0:T(8,128)(2,1)}, u32[]{:S(2)}, u32[]{:S(2)}) collective-permute-start(bf16[32,3072]{1,0:T(8,128)(2,1)} %pad_maximum_fusion.1), channel_id=1, source_target_pairs={{0,6},{2,4},{4,2},{6,0},{1,7},{3,5},{5,3},{7,1},{8,14},{10,12},{12... | collective-permute-start | bytes 589832 | tf_op jit(solution)/shard_map/ppermute | solution.py:35
  84.2 14.8 %all_gather.11.cols = bf16[4,8,4,16,192]{4,3,2,1,0:T(8,128)(2,1)S(1)} all-gather(bf16[1,8,4,16,192]{4,3,2,1,0:T(8,128)(2,1)} %bitcast.14), channel_id=1, replica_groups=mesh['gx'=8,'x'=4,'zh'=2,'yp'=2,'yl'=2,'core'=2] {'x'}, dimensions={0}, use_global_device_ids=true | all-gather | bytes 983040 | tf_op jit(solution)/shard_map/all_gather | solution.py:126
  99.3 7.5 %products.1 = (bf16[4,4,8,16,192]{4,3,2,1,0:T(8,128)(2,1)S(1)}, bf16[512,3072]{1,0:T(8,128)(2,1)}) custom-call(s32[8]{0:T(128)S(1)} %gather_fusion, s32[4]{0:T(128)S(1)} %pad_add_fusion.dest, bf16[32,3072]{1,0:T(8,128)(2,1)S(1)} %get-tuple-element.11.refs_0_, bf16[32,3072]{1,0:T(8,128)(2,1)S(1)} %collective-permute-done.refs_1_, ...), custom_call_target="tpu_custom_call" | custom-call | flops 2415919104 | bytes 12582912 | tf_op jit(solution)/shard_map/products/pallas_call | solution.py:128
  106.8 1.9 copy-done.2
  108.7 6.7 %weight_sums.1 = (f32[2,192,3072]{2,1,0:T(8,128)}, f32[2,192,3072]{2,1,0:T(8,128)}) custom-call(s32[8]{0:T(128)S(1)} %gather_fusion, s32[4]{0:T(128)S(1)} %pad_add_fusion.dest, bf16[4,8,4,16,192]{4,3,2,1,0:T(8,128)(2,1)S(1)} %all_gather.11.cols, bf16[512,3072]{1,0:T(8,128)(2,1)S(1)} %copy-done.2), custom_call_target="tpu_custom_call" | custom-call | flops 2415919104 | bytes 14680064 | tf_op jit(solution)/shard_map/weight_sums/pallas_call | solution.py:175
  115.4 1.9 collective-permute-start.14
  117.3 20.6 %all_to_all.15 = bf16[16,8,16,192]{3,2,1,0:T(8,128)(2,1)S(1)} all-to-all(bf16[16,8,16,192]{3,2,1,0:T(8,128)(2,1)S(1)} %bitcast.28), channel_id=1, replica_groups=mesh['gx'=8,'x'=4,'zh'=2,'yp'=2,'yl'=2,'core'=2] {'x','yl','core'}, dimensions={0} | all-to-all | bytes 1572864 | tf_op jit(solution)/shard_map/all_to_all | solution.py:143
  137.9 0.9 sum_x.1
  138.8 13.1 %all-to-all-start.1 = ((bf16[16,64,192]{2,1,0:T(8,128)(2,1)}), bf16[16,64,192]{2,1,0:T(8,128)(2,1)S(1)}, u32[]{:S(2)}, u32[]{:S(2)}) async-start(bf16[16,64,192]{2,1,0:T(8,128)(2,1)} %bitcast.8), calls=%async_computation.1 | async-start | bytes 1048576 | tf_op jit(solution)/shard_map/all_to_all | solution.py:154
  152.0 3.7 %fusion.4 = bf16[192,3072]{1,0:T(8,128)(2,1)} fusion(f32[2,192,3072]{2,1,0:T(8,128)} %collective-permute-done.14, f32[2,192,3072]{2,1,0:T(8,128)} %get-tuple-element.8), kind=kLoop, calls=%fused_computation.7 | loop fusion | flops 1179648 | bytes 5898240 | tf_op jit(solution)/shard_map/convert_element_type | solution.py:194
  155.6 3.5 %collective-permute-start.15 = (bf16[192,3072]{1,0:T(8,128)(2,1)}, bf16[192,3072]{1,0:T(8,128)(2,1)S(1)}, u32[]{:S(2)}, u32[]{:S(2)}) collective-permute-start(bf16[192,3072]{1,0:T(8,128)(2,1)} %fusion.4), channel_id=1, source_target_pairs={{0,2},{2,0},{1,3},{3,1},{4,6},{6,4},{5,7},{7,5},{8,10},{10,8},{9,1... | collective-permute-start | bytes 3538952 | tf_op jit(solution)/shard_map/ppermute | solution.py:31
  159.2 25.3 %all-to-all-done.1 = bf16[16,64,192]{2,1,0:T(8,128)(2,1)S(1)} async-done(((bf16[16,64,192]{2,1,0:T(8,128)(2,1)}), bf16[16,64,192]{2,1,0:T(8,128)(2,1)S(1)}, u32[]{:S(2)}, u32[]{:S(2)}) %all-to-all-start.1) | async-done | bytes 393248 | tf_op jit(solution)/shard_map/all_to_all | solution.py:154
  184.6 13.3 %all-gather = bf16[256,1536]{1,0:T(8,128)(2,1)S(1)} all-gather(bf16[64,1536]{1,0:T(8,128)(2,1)S(1)} %sum_z.1), channel_id=2, replica_groups=mesh['gx'=8,'x'=4,'zh'=2,'yp'=2,'yl'=2,'core'=2] {'x'}, dimensions={0}, use_global_device_ids=true | all-gather | bytes 983040 | tf_op jit(solution)/shard_map/all_gather | solution.py:165
  197.9 0.9 place.1
  198.9 3.9 %fusion.3 = bf16[192,3072]{1,0:T(8,128)(2,1)} fusion(f32[2,192,3072]{2,1,0:T(8,128)} %collective-permute-done.14, bf16[192,3072]{1,0:T(8,128)(2,1)S(1)} %collective-permute-done.15, f32[2,192,3072]{2,1,0:T(8,128)} %get-tuple-element.8), kind=kLoop, calls=%fused_computation.6 | loop fusion | flops 2359296 | bytes 7077888 | tf_op jit(solution)/shard_map/convert_element_type | solution.py:195
  (45 shorter events, 7.9 us)
Async XLA Ops:
  0.6 13.8 %copy-start = (bf16[256,1536]{1,0:T(8,128)(2,1)S(1)}, bf16[256,1536]{1,0:T(8,128)(2,1)}, u32[]{:S(2)}) copy-start(bf16[256,1536]{1,0:T(8,128)(2,1)} %param.7) | copy-start | bytes 2359300
  0.6 28.6 %copy-start.5 = (s32[8]{0:T(128)S(1)}, s32[8]{0:T(128)}, u32[]{:S(2)}) copy-start(s32[8]{0:T(128)} %constant.72.clone) | copy-start | bytes 100
  0.7 29.2 %copy-start.4 = (s32[8]{0:T(128)S(1)}, s32[8]{0:T(128)}, u32[]{:S(2)}) copy-start(s32[8]{0:T(128)} %constant.74.clone) | copy-start | bytes 100
  2.7 27.8 %collective-permute-start.1 = (bf16[32,3072]{1,0:T(8,128)(2,1)S(1)}, bf16[32,3072]{1,0:T(8,128)(2,1)S(1)}, u32[]{:S(2)}, u32[]{:S(2)}) collective-permute-start(bf16[32,3072]{1,0:T(8,128)(2,1)S(1)} %get-tuple-element.11.refs_0_), channel_id=1, source_target_pairs={{0,64},{128,0},{256,128},{384,256},{448,384},{320,448},{192,320},{... | collective-permute-start | bytes 589832 | tf_op jit(solution)/shard_map/ppermute | solution.py:27
  7.9 27.0 %collective-permute-start = (bf16[32,3072]{1,0:T(8,128)(2,1)S(1)}, bf16[32,3072]{1,0:T(8,128)(2,1)S(1)}, u32[]{:S(2)}, u32[]{:S(2)}) collective-permute-start(bf16[32,3072]{1,0:T(8,128)(2,1)S(1)} %get-tuple-element.11.refs_0_), channel_id=1, source_target_pairs={{0,128},{128,256},{256,384},{384,448},{448,320},{320,192},{192,64}... | collective-permute-start | bytes 589832 | tf_op jit(solution)/shard_map/ppermute | solution.py:27
  9.8 46.6 %collective-permute-start.11 = (bf16[192,3072]{1,0:T(8,128)(2,1)}, bf16[192,3072]{1,0:T(8,128)(2,1)}, u32[]{:S(2)}, u32[]{:S(2)}) collective-permute-start(bf16[192,3072]{1,0:T(8,128)(2,1)} %refs_12_.1), channel_id=1, source_target_pairs={{0,2},{2,0},{1,3},{3,1},{4,6},{6,4},{5,7},{7,5},{8,10},{10,8},{9,1... | collective-permute-start | bytes 3538952 | tf_op jit(solution)/shard_map/ppermute | solution.py:31
  12.5 86.8 %collective-permute-start.12 = (bf16[192,3072]{1,0:T(8,128)(2,1)}, bf16[192,3072]{1,0:T(8,128)(2,1)}, u32[]{:S(2)}, u32[]{:S(2)}) collective-permute-start(bf16[192,3072]{1,0:T(8,128)(2,1)} %refs_12_.1), channel_id=1, source_target_pairs={{0,1},{1,0},{2,3},{3,2},{4,5},{5,4},{6,7},{7,6},{8,9},{9,8},{10,11... | collective-permute-start | bytes 3538952 | tf_op jit(solution)/shard_map/ppermute | solution.py:31
  14.5 46.6 %copy-start.3 = (s32[8]{0:T(128)S(1)}, s32[8]{0:T(128)}, u32[]{:S(2)}) copy-start(s32[8]{0:T(128)} %constant.73.clone) | copy-start | bytes 100
  15.8 68.4 %all-to-all-start.2 = ((bf16[32,16,192]{2,1,0:T(8,128)(2,1)}), bf16[32,16,192]{2,1,0:T(8,128)(2,1)}, u32[]{:S(2)}, u32[]{:S(2)}) async-start(bf16[32,16,192]{2,1,0:T(8,128)(2,1)} %bitcast.13), calls=%async_computation.2 | async-start | bytes 524288 | tf_op jit(solution)/shard_map/all_to_all | solution.py:125
  30.6 16.2 %collective-permute-start.3 = (bf16[32,3072]{1,0:T(8,128)(2,1)S(1)}, bf16[32,3072]{1,0:T(8,128)(2,1)S(1)}, u32[]{:S(2)}, u32[]{:S(2)}) collective-permute-start(bf16[32,3072]{1,0:T(8,128)(2,1)S(1)} %collective-permute-done.1.refs_2_), channel_id=1, source_target_pairs={{0,64},{128,0},{256,128},{384,256},{448,384},{320,448},{192,320},{... | collective-permute-start | bytes 589832 | tf_op jit(solution)/shard_map/ppermute | solution.py:27
  34.8 19.0 %collective-permute-start.2 = (bf16[32,3072]{1,0:T(8,128)(2,1)S(1)}, bf16[32,3072]{1,0:T(8,128)(2,1)S(1)}, u32[]{:S(2)}, u32[]{:S(2)}) collective-permute-start(bf16[32,3072]{1,0:T(8,128)(2,1)S(1)} %collective-permute-done.refs_1_), channel_id=1, source_target_pairs={{0,128},{128,256},{256,384},{384,448},{448,320},{320,192},{192,64}... | collective-permute-start | bytes 589832 | tf_op jit(solution)/shard_map/ppermute | solution.py:27
  37.5 61.8 %copy-start.1 = (bf16[192,3072]{1,0:T(8,128)(2,1)S(1)}, bf16[192,3072]{1,0:T(8,128)(2,1)}, u32[]{:S(2)}) copy-start(bf16[192,3072]{1,0:T(8,128)(2,1)} %refs_12_.1) | copy-start | bytes 3538948
  46.7 15.0 %collective-permute-start.5 = (bf16[32,3072]{1,0:T(8,128)(2,1)S(1)}, bf16[32,3072]{1,0:T(8,128)(2,1)S(1)}, u32[]{:S(2)}, u32[]{:S(2)}) collective-permute-start(bf16[32,3072]{1,0:T(8,128)(2,1)S(1)} %collective-permute-done.3.refs_4_), channel_id=1, source_target_pairs={{0,64},{128,0},{256,128},{384,256},{448,384},{320,448},{192,320},{... | collective-permute-start | bytes 589832 | tf_op jit(solution)/shard_map/ppermute | solution.py:27
  53.8 15.0 %collective-permute-start.4 = (bf16[32,3072]{1,0:T(8,128)(2,1)S(1)}, bf16[32,3072]{1,0:T(8,128)(2,1)S(1)}, u32[]{:S(2)}, u32[]{:S(2)}) collective-permute-start(bf16[32,3072]{1,0:T(8,128)(2,1)S(1)} %collective-permute-done.2.refs_3_), channel_id=1, source_target_pairs={{0,128},{128,256},{256,384},{384,448},{448,320},{320,192},{192,64}... | collective-permute-start | bytes 589832 | tf_op jit(solution)/shard_map/ppermute | solution.py:27
  56.4 42.8 %collective-permute-start.13 = (bf16[192,3072]{1,0:T(8,128)(2,1)}, bf16[192,3072]{1,0:T(8,128)(2,1)}, u32[]{:S(2)}, u32[]{:S(2)}) collective-permute-start(bf16[192,3072]{1,0:T(8,128)(2,1)} %collective-permute-done.11.refs_13_), channel_id=1, source_target_pairs={{0,1},{1,0},{2,3},{3,2},{4,5},{5,4},{6,7},{7,6},{8,9},{9,8},{10,11... | collective-permute-start | bytes 3538952 | tf_op jit(solution)/shard_map/ppermute | solution.py:31
  59.1 40.2 %collective-permute-start.8 = (bf16[160,3072]{1,0:T(8,128)(2,1)}, bf16[160,3072]{1,0:T(8,128)(2,1)}, u32[]{:S(2)}, u32[]{:S(2)}) collective-permute-start(bf16[160,3072]{1,0:T(8,128)(2,1)} %constant_dynamic-update-slice_fusion), channel_id=1, source_target_pairs={{0,6},{2,4},{4,2},{6,0},{1,7},{3,5},{5,3},{7,1},{8,14},{10,12},{12... | collective-permute-start | bytes 2949128 | tf_op jit(solution)/shard_map/ppermute | solution.py:35
  61.7 9.8 %collective-permute-start.7 = (bf16[16,3072]{1,0:T(8,128)(2,1)S(1)}, bf16[16,3072]{1,0:T(8,128)(2,1)S(1)}, u32[]{:S(2)}, u32[]{:S(2)}) collective-permute-start(bf16[16,3072]{1,0:T(8,128)(2,1)S(1)} %slice.35), channel_id=1, source_target_pairs={{0,64},{128,0},{256,128},{384,256},{448,384},{320,448},{192,320},{... | collective-permute-start | bytes 294920 | tf_op jit(solution)/shard_map/ppermute | solution.py:27
  68.9 9.8 %collective-permute-start.6 = (bf16[16,3072]{1,0:T(8,128)(2,1)S(1)}, bf16[16,3072]{1,0:T(8,128)(2,1)S(1)}, u32[]{:S(2)}, u32[]{:S(2)}) collective-permute-start(bf16[16,3072]{1,0:T(8,128)(2,1)S(1)} %slice.34), channel_id=1, source_target_pairs={{0,128},{128,256},{256,384},{384,448},{448,320},{320,192},{192,64}... | collective-permute-start | bytes 294920 | tf_op jit(solution)/shard_map/ppermute | solution.py:27
  71.6 27.7 %collective-permute-start.9 = (bf16[64,3072]{1,0:T(8,128)(2,1)}, bf16[64,3072]{1,0:T(8,128)(2,1)}, u32[]{:S(2)}, u32[]{:S(2)}) collective-permute-start(bf16[64,3072]{1,0:T(8,128)(2,1)} %pad_maximum_fusion), channel_id=1, source_target_pairs={{0,6},{2,4},{4,2},{6,0},{1,7},{3,5},{5,3},{7,1},{8,14},{10,12},{12... | collective-permute-start | bytes 1179656 | tf_op jit(solution)/shard_map/ppermute | solution.py:35
  79.3 20.0 %collective-permute-start.10 = (bf16[32,3072]{1,0:T(8,128)(2,1)}, bf16[32,3072]{1,0:T(8,128)(2,1)}, u32[]{:S(2)}, u32[]{:S(2)}) collective-permute-start(bf16[32,3072]{1,0:T(8,128)(2,1)} %pad_maximum_fusion.1), channel_id=1, source_target_pairs={{0,6},{2,4},{4,2},{6,0},{1,7},{3,5},{5,3},{7,1},{8,14},{10,12},{12... | collective-permute-start | bytes 589832 | tf_op jit(solution)/shard_map/ppermute | solution.py:35
  106.8 1.9 copy-start.2
  115.4 36.6 %collective-permute-start.14 = (f32[2,192,3072]{2,1,0:T(8,128)}, f32[2,192,3072]{2,1,0:T(8,128)}, u32[]{:S(2)}, u32[]{:S(2)}) collective-permute-start(f32[2,192,3072]{2,1,0:T(8,128)} %get-tuple-element.9), channel_id=1, source_target_pairs={{0,1},{1,0},{2,3},{3,2},{4,5},{5,4},{6,7},{7,6},{8,9},{9,8},{10,11... | collective-permute-start | bytes 14155784 | tf_op jit(solution)/shard_map/ppermute | solution.py:31
  138.8 45.7 %all-to-all-start.1 = ((bf16[16,64,192]{2,1,0:T(8,128)(2,1)}), bf16[16,64,192]{2,1,0:T(8,128)(2,1)S(1)}, u32[]{:S(2)}, u32[]{:S(2)}) async-start(bf16[16,64,192]{2,1,0:T(8,128)(2,1)} %bitcast.8), calls=%async_computation.1 | async-start | bytes 1048576 | tf_op jit(solution)/shard_map/all_to_all | solution.py:154
  155.6 43.2 %collective-permute-start.15 = (bf16[192,3072]{1,0:T(8,128)(2,1)}, bf16[192,3072]{1,0:T(8,128)(2,1)S(1)}, u32[]{:S(2)}, u32[]{:S(2)}) collective-permute-start(bf16[192,3072]{1,0:T(8,128)(2,1)} %fusion.4), channel_id=1, source_target_pairs={{0,2},{2,0},{1,3},{3,1},{4,6},{6,4},{5,7},{7,5},{8,10},{10,8},{9,1... | collective-permute-start | bytes 3538952 | tf_op jit(solution)/shard_map/ppermute | solution.py:31

commit v3 on v2

v3 whole, which is shorter than its diff:
```python
import functools

import jax
import jax.numpy as jnp
from jax import lax
from jax.experimental import pallas as pl
from jax.experimental.pallas import tpu as pltpu
from jax.sharding import Mesh
from jax.sharding import PartitionSpec as P

RING = (0, 2, 4, 6, 7, 5, 3, 1)
STEPS = (0, -1, 1, -2, 2, -3, 3, 4)
F32 = jnp.float32
BF16 = jnp.bfloat16
VMEM = pl.BlockSpec(memory_space=pltpu.VMEM)
LIMIT = pltpu.CompilerParams(vmem_limit_bytes=48 * 1024 * 1024)
TILE = 768


def gelu_slope(value):
    scale = 0.7978845608028654
    tangent = jnp.tanh(scale * (value + 0.044715 * value * value * value))
    inner = scale * (1.0 + 3.0 * 0.044715 * value * value)
    return 0.5 * (1.0 + tangent) + 0.5 * value * (1.0 - tangent * tangent) * inner


def hop(value, step):
    return lax.ppermute(value, "gx", [(RING[q], RING[(q + step) % 8]) for q in range(8)])


def swap(value, axis):
    return lax.ppermute(value, axis, [(0, 1), (1, 0)])


def across(value):
    return lax.ppermute(value, ("yp", "yl"), [(k, 3 - k) for k in range(4)])


def owners():
    gx = lax.axis_index("gx")
    place = jnp.where(lax.rem(gx, 2) == 0, gx // 2, 7 - gx // 2)
    found = []
    for step in STEPS:
        q = lax.rem(place + step + 8, 8)
        found.append(jnp.where(q < 4, 2 * q, 15 - 2 * q))
    return found


def dests():
    yl, core = lax.axis_index("yl"), lax.axis_index("core")
    return [a * 2 + b for b in (core, 1 - core) for a in (yl, 1 - yl)]


def part_kernel(inputs, out):
    xp, xl, yp = (lax.axis_index(a) for a in ("xp", "xl", "yp"))
    for a in range(2):
        for c in range(2):
            y = jnp.where(xp == 0, yp * 2 + a, 3 - yp * 2 - a)
            block = inputs[pl.ds(pl.multiple_of(y * 64 + c * 32 + xl * 16, 16), 16)]
            for k in range(8):
                out[k * 4 + a * 2 + c] = block[:, k * 192 : (k + 1) * 192]


def product_kernel(*refs):
    pieces, weights, (rows, whole) = refs[:12], refs[12:16], refs[16:]
    owner, dest = owners(), dests()
    at = 0
    for piece in pieces:
        whole[at : at + piece.shape[0]] = piece[...]
        at += piece.shape[0]
    for j, weight in enumerate(weights):
        block = lax.dot_general(
            whole[...], weight[...], (((1,), (1,)), ((), ())), preferred_element_type=F32
        ).astype(BF16)
        for first in range(0, 512, 16):
            side, slot, half = first // 256, first // 32 % 8, first // 16 % 2
            rows[side * 2 + half, dest[j], owner[slot]] = block[first : first + 16]


def weight_kernel(j0, *refs):
    cols, (whole, out, held, turned) = refs[:3], refs[3:]

    @pl.when(pl.program_id(0) == 0)
    def _():
        own_x = lax.axis_index("xp") * 2 + lax.axis_index("xl")
        owner, dest = owners(), dests()
        held[own_x] = cols[0][...]
        held[own_x ^ 1] = cols[1][...]
        held[own_x ^ 2] = cols[2][0]
        held[own_x ^ 3] = cols[2][1]
        for j in range(2):
            parts = [
                held[side * 2 + half, owner[slot], dest[j0 + j]]
                for side in range(2)
                for slot in range(8)
                for half in range(2)
            ]
            turned[j * 192 : (j + 1) * 192] = jnp.concatenate(parts, 0).T

    total = jnp.dot(turned[...], whole[...], preferred_element_type=F32)
    for j in range(2):
        out[j] = total[j * 192 : (j + 1) * 192].astype(out.dtype)


def weight_sums(j0, dtype, cols, whole):
    part = pl.BlockSpec((8, 4, 16, 192), lambda i: (0, 0, 0, 0))
    return pl.pallas_call(
        functools.partial(weight_kernel, j0),
        grid=(3072 // TILE,),
        out_shape=jax.ShapeDtypeStruct((2, 192, 3072), dtype),
        in_specs=[part, part, pl.BlockSpec((2, 8, 4, 16, 192), lambda i: (0, 0, 0, 0, 0))]
        + [pl.BlockSpec((512, TILE), lambda i: (0, i))],
        out_specs=pl.BlockSpec((2, 192, TILE), lambda i: (0, 0, i)),
        scratch_shapes=[pltpu.VMEM((4, 8, 4, 16, 192), BF16), pltpu.VMEM((384, 512), BF16)],
        compiler_params=LIMIT,
        cost_estimate=pl.CostEstimate(
            flops=512 * 3072 * 768, bytes_accessed=8 << 20, transcendentals=0
        ),
        name="weight_sums",
    )(*cols, whole)


def add_kernel(parts, out):
    for k in range(8):
        for j in range(4):
            total = parts[0, j, k].astype(F32)
            for i in range(1, 4):
                total = total + parts[i, j, k].astype(F32)
            total = total.astype(BF16)
            out[k, 0, j] = total
            out[k, 1, j] = total


def pair_kernel(parts, out):
    sums = [parts[k, 0].astype(F32) + parts[k, 1].astype(F32) for k in range(8)]
    out[...] = jnp.concatenate(sums, 1).astype(BF16)


def place_kernel(parts, out):
    mine = lax.axis_index("yp")
    for p in range(2):
        side = jnp.where(mine == p, 0, 1)
        for s in range(2):
            source = jnp.where(mine == p, s, 1 - s)
            for c in range(2):
                for half in range(2):
                    first = p * 128 + s * 64 + c * 32 + half * 16
                    out[first : first + 16] = parts[side * 2 + half, source * 2 + c]


def meet_kernel(keep, met, own, passed):
    own[...] = keep[0] + met[0].astype(F32)
    passed[...] = (keep[1] + met[1].astype(F32)).astype(BF16)


def close_kernel(own, passed, out):
    out[...] = (own[...] + passed[...].astype(F32)).astype(BF16)


def whole_call(kernel, shape, name):
    return pl.pallas_call(
        kernel,
        out_shape=jax.ShapeDtypeStruct(shape, BF16),
        in_specs=[VMEM],
        out_specs=VMEM,
        compiler_params=LIMIT,
        name=name,
    )


def shards(inputs, weight, grad_out, pre_act):
    gh = (grad_out.astype(F32) * gelu_slope(pre_act.astype(F32))).astype(BF16)

    part = whole_call(part_kernel, (32, 16, 192), "part")(inputs)
    part, gh = lax.optimization_barrier((part, gh))
    part = lax.all_to_all(part, ("gx", "yl", "core"), split_axis=0, concat_axis=0, tiled=True)
    part = part.reshape(8, 4, 16, 192)

    up, down, far = [gh], [gh], []
    for s in range(3):
        up.append(hop(up[-1], 1))
        far.append(across(jnp.concatenate([down[-1], up[-1]], 0)))
        down.append(hop(down[-1], -1))
        if s == 0:
            up[1], down[1], part = lax.optimization_barrier((up[1], down[1], part))
            beside_x = swap(part, "xl")
        if s == 1:
            up[2], down[2], far[0] = lax.optimization_barrier((up[2], down[2], far[0]))
        if s == 2:
            up[3], down[3], far[1], beside_x = lax.optimization_barrier(
                (up[3], down[3], far[1], beside_x)
            )
            cols = (part, beside_x, swap(jnp.stack([part, beside_x], 0), "xp"))
    up.append(hop(up[3], 1))
    far.append(across(jnp.concatenate([down[3], up[4]], 0)))

    beside = swap(weight, "yl")
    weight, beside, up[2] = lax.optimization_barrier((weight, beside, up[2]))
    weights = (weight, beside, swap(weight, "core"), swap(beside, "core"))

    rows, whole = pl.pallas_call(
        product_kernel,
        out_shape=(
            jax.ShapeDtypeStruct((4, 4, 8, 16, 192), BF16),
            jax.ShapeDtypeStruct((512, 3072), BF16),
        ),
        in_specs=[VMEM] * 16,
        out_specs=(VMEM,) * 2,
        compiler_params=LIMIT,
        cost_estimate=pl.CostEstimate(
            flops=2 * 512 * 3072 * 768, bytes_accessed=12 << 20, transcendentals=0
        ),
        name="products",
    )(gh, up[1], down[1], up[2], down[2], up[3], down[3], up[4], *far, *weights)

    send = weight_sums(2, BF16, cols, whole)

    rows = lax.all_to_all(
        rows.reshape(16, 8, 16, 192),
        ("xp", "xl", "yl", "core"),
        split_axis=0,
        concat_axis=0,
        tiled=True,
    )
    rows, whole = lax.optimization_barrier((rows, whole))
    keep = weight_sums(0, F32, cols, whole)
    rows = whole_call(add_kernel, (8, 2, 4, 16, 192), "sum_x")(rows.reshape(4, 4, 8, 16, 192))
    rows = lax.all_to_all(
        rows.reshape(16, 64, 192), ("gx", "zh"), split_axis=0, concat_axis=0, tiled=True
    )
    rows = whole_call(pair_kernel, (64, 1536), "sum_z")(rows.reshape(8, 2, 64, 192))
    rows = lax.all_gather(rows, ("xp", "xl"), axis=0)
    grad_in = whole_call(place_kernel, (256, 1536), "place")(rows.reshape(4, 4, 16, 1536))

    met = swap(send, "core")
    pair = pl.BlockSpec((2, 192, TILE), lambda i: (0, 0, i))
    one = pl.BlockSpec((192, TILE), lambda i: (0, i))
    own, passed = pl.pallas_call(
        meet_kernel,
        grid=(3072 // TILE,),
        out_shape=(
            jax.ShapeDtypeStruct((192, 3072), F32),
            jax.ShapeDtypeStruct((192, 3072), BF16),
        ),
        in_specs=[pair, pair],
        out_specs=(one, one),
        compiler_params=LIMIT,
        name="meet",
    )(keep, met)
    grad_weight = pl.pallas_call(
        close_kernel,
        grid=(3072 // TILE,),
        out_shape=jax.ShapeDtypeStruct((192, 3072), BF16),
        in_specs=[one, one],
        out_specs=one,
        compiler_params=LIMIT,
        name="close",
    )(own, swap(passed, "yl"))
    return grad_in, grad_weight


def solution(mesh):
    names = ("gx", "xp", "xl", "zh", "yp", "yl", "core")
    fine = Mesh(mesh.devices.reshape(8, 2, 2, 2, 2, 2, 2), names)
    split = P(("gx", "yp", "yl", "core"), ("xp", "xl", "zh"))
    tokens = P("gx", ("yp", "yl", "core"))
    rows = P(("yp", "yl", "core", "gx"), ("xp", "xl", "zh"))
    return jax.shard_map(
        shards,
        mesh=fine,
        in_specs=(tokens, rows, split, split),
        out_specs=(tokens, rows),
        check_vma=False,
    )
```

time: 204 us -> 198 us (0.971)
  the two profiles are of different devices: /device:TPU:56 before, /device:TPU:32 now
where the time goes in v3:
time: 198 us; the launch traced here: 197 us
  starting transfers between devices  84.6 us (43%)
  waiting for transfers between devices  43.4 us (22%)
  blocking collectives  34.1 us (17%)
  Pallas kernels  26.4 us (13%)
  local copies, waits for them, and re-layouts  6.02 us (3%)
    ppermute x7, starting transfers between devices, hop(): lax.ppermute(value, 'gx', [(RING[q], RING[(q + step) % 8]) for q in range...  28.5 us
    all_to_all x1, blocking collectives, shards(): lax.all_to_all(rows.reshape(16, 8, 16, 192), ('xp', 'xl', 'yl', 'core'),...  20.8 us
    ppermute x7, starting transfers between devices, swap(): return lax.ppermute(value, axis, [(0, 1), (1, 0)])  19.9 us
    all_to_all x1, waiting for transfers between devices, shards(): lax.all_to_all(rows.reshape(16, 64, 192), ('gx', 'zh'), split_axis=0, con...  18.5 us
    ppermute x7, waiting for transfers between devices, hop(): lax.ppermute(value, 'gx', [(RING[q], RING[(q + step) % 8]) for q in range...  18 us
    all_to_all x1, starting transfers between devices, shards(): lax.all_to_all(part, ('gx', 'yl', 'core'), split_axis=0, concat_axis=0, t...  13.8 us
    all_gather x1, blocking collectives, shards(): rows = lax.all_gather(rows, ('xp', 'xl'), axis=0)  13.3 us
    ppermute x4, starting transfers between devices, across(): return lax.ppermute(value, ('yp', 'yl'), [(k, 3 - k) for k in range(4)])  12.3 us
  transfers between devices with their start and end apart: 20, of which 6 were waited for; matrix products, arithmetic and copies ran while one was open for 0% of the time, Pallas kernels for 8%

profile of v3, /device:TPU:32, one launch (start us, length us, event | category | flops | bytes accessed | tf_op | source)
XLA Modules:
  0.0 196.9 jit_solution(1674262932756068922)
XLA Ops:
  3.9 13.8 %all-to-all-start = ((bf16[32,16,192]{2,1,0:T(8,128)(2,1)}), bf16[32,16,192]{2,1,0:T(8,128)(2,1)S(1)}, u32[]{:S(2)}, u32[]{:S(2)}) async-start(bf16[32,16,192]{2,1,0:T(8,128)(2,1)} %part.1), calls=%async_computation | async-start | bytes 524288 | tf_op jit(solution)/shard_map/all_to_all | solution.py:176
  17.7 4.3 %collective-permute-start.1 = (bf16[32,3072]{1,0:T(8,128)(2,1)S(1)}, bf16[32,3072]{1,0:T(8,128)(2,1)S(1)}, u32[]{:S(2)}, u32[]{:S(2)}) collective-permute-start(bf16[32,3072]{1,0:T(8,128)(2,1)S(1)} %fusion.6.refs_0_), channel_id=1, source_target_pairs={{0,64},{128,0},{256,128},{384,256},{448,384},{320,448},{192,320},{... | collective-permute-start | bytes 589832 | tf_op jit(solution)/shard_map/ppermute | solution.py:28
  22.0 1.9 collective-permute-start
  23.9 3.4 %collective-permute-start.2 = (bf16[192,3072]{1,0:T(8,128)(2,1)S(1)}, bf16[192,3072]{1,0:T(8,128)(2,1)S(1)}, u32[]{:S(2)}, u32[]{:S(2)}) collective-permute-start(bf16[192,3072]{1,0:T(8,128)(2,1)S(1)} %copy-done.7), channel_id=1, source_target_pairs={{0,2},{2,0},{1,3},{3,1},{4,6},{6,4},{5,7},{7,5},{8,10},{10,8},{9,1... | collective-permute-start | bytes 3538952 | tf_op jit(solution)/shard_map/ppermute | solution.py:32
  27.3 7.7 %collective-permute-done.1.refs_2_ = bf16[32,3072]{1,0:T(8,128)(2,1)S(1)} collective-permute-done((bf16[32,3072]{1,0:T(8,128)(2,1)S(1)}, bf16[32,3072]{1,0:T(8,128)(2,1)S(1)}, u32[]{:S(2)}, u32[]{:S(2)}) %collective-permute-start.1) | collective-permute-done | bytes 196640 | tf_op jit(solution)/shard_map/ppermute | solution.py:28
  35.0 4.0 %collective-permute-done.refs_1_ = bf16[32,3072]{1,0:T(8,128)(2,1)S(1)} collective-permute-done((bf16[32,3072]{1,0:T(8,128)(2,1)S(1)}, bf16[32,3072]{1,0:T(8,128)(2,1)S(1)}, u32[]{:S(2)}, u32[]{:S(2)}) %collective-permute-start) | collective-permute-done | bytes 196640 | tf_op jit(solution)/shard_map/ppermute | solution.py:28
  39.1 1.9 collective-permute-start.3
  41.0 4.7 %collective-permute-start.5 = (bf16[64,3072]{1,0:T(8,128)(2,1)S(1)}, bf16[64,3072]{1,0:T(8,128)(2,1)S(1)}, u32[]{:S(2)}, u32[]{:S(2)}) collective-permute-start(bf16[64,3072]{1,0:T(8,128)(2,1)S(1)} %pad_maximum_fusion.1), channel_id=1, source_target_pairs={{0,6},{2,4},{4,2},{6,0},{1,7},{3,5},{5,3},{7,1},{8,14},{10,12},{12... | collective-permute-start | bytes 1179656 | tf_op jit(solution)/shard_map/ppermute | solution.py:36
  45.8 6.6 %collective-permute-start.4 = (bf16[32,3072]{1,0:T(8,128)(2,1)S(1)}, bf16[32,3072]{1,0:T(8,128)(2,1)S(1)}, u32[]{:S(2)}, u32[]{:S(2)}) collective-permute-start(bf16[32,3072]{1,0:T(8,128)(2,1)S(1)} %collective-permute-done.1.refs_2_), channel_id=1, source_target_pairs={{0,64},{128,0},{256,128},{384,256},{448,384},{320,448},{192,320},{... | collective-permute-start | bytes 589832 | tf_op jit(solution)/shard_map/ppermute | solution.py:28
  52.5 2.7 %collective-permute-start.8 = (bf16[64,3072]{1,0:T(8,128)(2,1)S(1)}, bf16[64,3072]{1,0:T(8,128)(2,1)S(1)}, u32[]{:S(2)}, u32[]{:S(2)}) collective-permute-start(bf16[64,3072]{1,0:T(8,128)(2,1)S(1)} %pad_maximum_fusion.2), channel_id=1, source_target_pairs={{0,6},{2,4},{4,2},{6,0},{1,7},{3,5},{5,3},{7,1},{8,14},{10,12},{12... | collective-permute-start | bytes 1179656 | tf_op jit(solution)/shard_map/ppermute | solution.py:36
  55.2 3.4 %collective-permute-start.9 = (bf16[8,4,16,192]{3,2,1,0:T(8,128)(2,1)S(1)}, bf16[8,4,16,192]{3,2,1,0:T(8,128)(2,1)S(1)}, u32[]{:S(2)}, u32[]{:S(2)}) collective-permute-start(bf16[8,4,16,192]{3,2,1,0:T(8,128)(2,1)S(1)} %bitcast.8), channel_id=1, source_target_pairs={{0,16},{16,0},{1,17},{17,1},{2,18},{18,2},{3,19},{19,3},{4,20},{20... | collective-permute-start | bytes 589832 | tf_op jit(solution)/shard_map/ppermute | solution.py:32
  58.6 4.3 %collective-permute-start.6 = (bf16[32,3072]{1,0:T(8,128)(2,1)S(1)}, bf16[32,3072]{1,0:T(8,128)(2,1)S(1)}, u32[]{:S(2)}, u32[]{:S(2)}) collective-permute-start(bf16[32,3072]{1,0:T(8,128)(2,1)S(1)} %collective-permute-done.3.refs_3_), channel_id=1, source_target_pairs={{0,128},{128,256},{256,384},{384,448},{448,320},{320,192},{192,64}... | collective-permute-start | bytes 589832 | tf_op jit(solution)/shard_map/ppermute | solution.py:28
  62.9 7.6 %collective-permute-start.7 = (bf16[32,3072]{1,0:T(8,128)(2,1)S(1)}, bf16[32,3072]{1,0:T(8,128)(2,1)S(1)}, u32[]{:S(2)}, u32[]{:S(2)}) collective-permute-start(bf16[32,3072]{1,0:T(8,128)(2,1)S(1)} %collective-permute-done.4.refs_4_), channel_id=1, source_target_pairs={{0,64},{128,0},{256,128},{384,256},{448,384},{320,448},{192,320},{... | collective-permute-start | bytes 589832 | tf_op jit(solution)/shard_map/ppermute | solution.py:28
  70.5 1.9 collective-permute-start.13
  72.5 2.4 %collective-permute-start.14 = (bf16[192,3072]{1,0:T(8,128)(2,1)S(1)}, bf16[192,3072]{1,0:T(8,128)(2,1)S(1)}, u32[]{:S(2)}, u32[]{:S(2)}) collective-permute-start(bf16[192,3072]{1,0:T(8,128)(2,1)S(1)} %collective-permute-done.2.refs_13_), channel_id=1, source_target_pairs={{0,1},{1,0},{2,3},{3,2},{4,5},{5,4},{6,7},{7,6},{8,9},{9,8},{10,11... | collective-permute-start | bytes 3538952 | tf_op jit(solution)/shard_map/ppermute | solution.py:32
  75.2 1.9 collective-permute-start.10
  77.1 3.0 %collective-permute-start.11 = (bf16[64,3072]{1,0:T(8,128)(2,1)S(1)}, bf16[64,3072]{1,0:T(8,128)(2,1)S(1)}, u32[]{:S(2)}, u32[]{:S(2)}) collective-permute-start(bf16[64,3072]{1,0:T(8,128)(2,1)S(1)} %pad_maximum_fusion.3), channel_id=1, source_target_pairs={{0,6},{2,4},{4,2},{6,0},{1,7},{3,5},{5,3},{7,1},{8,14},{10,12},{12... | collective-permute-start | bytes 1179656 | tf_op jit(solution)/shard_map/ppermute | solution.py:36
  80.1 5.9 %collective-permute-done.10.refs_7_ = bf16[32,3072]{1,0:T(8,128)(2,1)S(1)} collective-permute-done((bf16[32,3072]{1,0:T(8,128)(2,1)S(1)}, bf16[32,3072]{1,0:T(8,128)(2,1)S(1)}, u32[]{:S(2)}, u32[]{:S(2)}) %collective-permute-start.10) | collective-permute-done | bytes 196640 | tf_op jit(solution)/shard_map/ppermute | solution.py:28
  86.1 1.9 collective-permute-start.12
  88.1 4.6 %collective-permute-start.15 = (bf16[2,8,4,16,192]{4,3,2,1,0:T(8,128)(2,1)S(1)}, bf16[2,8,4,16,192]{4,3,2,1,0:T(8,128)(2,1)S(1)}, u32[]{:S(2)}, u32[]{:S(2)}) collective-permute-start(bf16[2,8,4,16,192]{4,3,2,1,0:T(8,128)(2,1)S(1)} %pad_maximum_fusion), channel_id=1, source_target_pairs={{0,32},{32,0},{1,33},{33,1},{2,34},{34,2},{3,35},{35,3},{4,36},{36... | collective-permute-start | bytes 1179656 | tf_op jit(solution)/shard_map/ppermute | solution.py:32
  92.8 6.9 %collective-permute-done.12.refs_11_ = bf16[64,3072]{1,0:T(8,128)(2,1)S(1)} collective-permute-done((bf16[64,3072]{1,0:T(8,128)(2,1)S(1)}, bf16[64,3072]{1,0:T(8,128)(2,1)S(1)}, u32[]{:S(2)}, u32[]{:S(2)}) %collective-permute-start.12) | collective-permute-done | bytes 393248 | tf_op jit(solution)/shard_map/ppermute | solution.py:36
  101.8 5.4 %products.1 = (bf16[4,4,8,16,192]{4,3,2,1,0:T(8,128)(2,1)S(1)}, bf16[512,3072]{1,0:T(8,128)(2,1)}) custom-call(bf16[32,3072]{1,0:T(8,128)(2,1)S(1)} %fusion.6.refs_0_, bf16[32,3072]{1,0:T(8,128)(2,1)S(1)} %collective-permute-done.refs_1_, bf16[32,3072]{1,0:T(8,128)(2,1)S(1)} %collective-permute-done.1.refs_2_, ...), custom_call_target="tpu_custom_call" | custom-call | flops 2415919104 | bytes 12582912 | tf_op jit(solution)/shard_map/products/pallas_call | solution.py:201
  107.2 5.6 %weight_sums.3 = bf16[2,192,3072]{2,1,0:T(8,128)(2,1)} custom-call(bf16[8,4,16,192]{3,2,1,0:T(8,128)(2,1)S(1)} %bitcast.10, bf16[8,4,16,192]{3,2,1,0:T(8,128)(2,1)S(1)} %collective-permute-done.9.refs_1_, bf16[2,8,4,16,192]{4,3,2,1,0:T(8,128)(2,1)S(1)} %collective-permute-done.15.refs_2_, bf16[512,3072]{1,0:T(8,128)(2,1)} %get-tuple-element.41.refs_3_), custom_call_target="tpu_custom_call" | custom-call | flops 1207959552 | bytes 8388608 | tf_op jit(solution)/shard_map/weight_sums/pallas_call | solution.py:107
  112.8 1.9 collective-permute-start.16
  114.7 20.8 %all_to_all.15 = bf16[16,8,16,192]{3,2,1,0:T(8,128)(2,1)S(1)} all-to-all(bf16[16,8,16,192]{3,2,1,0:T(8,128)(2,1)S(1)} %bitcast.16), channel_id=1, replica_groups=mesh['gx'=8,'xp'=2,'xl'=2,'zh'=2,'yp'=2,'yl'=2,'core'=2] {'xp','xl','yl'..., dimensions={0} | all-to-all | bytes 1572864 | tf_op jit(solution)/shard_map/all_to_all | solution.py:218
  136.4 10.0 %all-to-all-start.2 = ((bf16[16,64,192]{2,1,0:T(8,128)(2,1)}), bf16[16,64,192]{2,1,0:T(8,128)(2,1)}, u32[]{:S(2)}, u32[]{:S(2)}) async-start(bf16[16,64,192]{2,1,0:T(8,128)(2,1)} %bitcast.15), calls=%async_computation.2 | async-start | bytes 1048576 | tf_op jit(solution)/shard_map/all_to_all | solution.py:228
  148.4 4.1 %weight_sums.2.keep = f32[2,192,3072]{2,1,0:T(8,128)} custom-call(bf16[8,4,16,192]{3,2,1,0:T(8,128)(2,1)S(1)} %bitcast.11, bf16[8,4,16,192]{3,2,1,0:T(8,128)(2,1)S(1)} %copy-done.2, bf16[2,8,4,16,192]{4,3,2,1,0:T(8,128)(2,1)S(1)} %copy-done.4, bf16[512,3072]{1,0:T(8,128)(2,1)S(1)} %copy-done), custom_call_target="tpu_custom_call" | custom-call | flops 1207959552 | bytes 8388608 | tf_op jit(solution)/shard_map/weight_sums/pallas_call | solution.py:107
  152.5 4.7 %meet.1 = (f32[192,3072]{1,0:T(8,128)S(1)}, bf16[192,3072]{1,0:T(8,128)(2,1)}) custom-call(f32[2,192,3072]{2,1,0:T(8,128)} %weight_sums.2.keep, bf16[2,192,3072]{2,1,0:T(8,128)(2,1)} %collective-permute-done.16.met), custom_call_target="tpu_custom_call" | custom-call | tf_op jit(solution)/shard_map/meet/pallas_call | solution.py:238
  157.2 2.3 %collective-permute-start.17 = (bf16[192,3072]{1,0:T(8,128)(2,1)}, bf16[192,3072]{1,0:T(8,128)(2,1)}, u32[]{:S(2)}, u32[]{:S(2)}) collective-permute-start(bf16[192,3072]{1,0:T(8,128)(2,1)} %get-tuple-element.43), channel_id=1, source_target_pairs={{0,2},{2,0},{1,3},{3,1},{4,6},{6,4},{5,7},{7,5},{8,10},{10,8},{9,1... | collective-permute-start | bytes 3538952 | tf_op jit(solution)/shard_map/ppermute | solution.py:32
  159.5 18.5 %all-to-all-done.2 = bf16[16,64,192]{2,1,0:T(8,128)(2,1)} async-done(((bf16[16,64,192]{2,1,0:T(8,128)(2,1)}), bf16[16,64,192]{2,1,0:T(8,128)(2,1)}, u32[]{:S(2)}, u32[]{:S(2)}) %all-to-all-start.2) | async-done | bytes 393248 | tf_op jit(solution)/shard_map/all_to_all | solution.py:228
  179.1 13.3 %all-gather = bf16[256,1536]{1,0:T(8,128)(2,1)S(1)} all-gather(bf16[64,1536]{1,0:T(8,128)(2,1)S(1)} %sum_z.1), channel_id=2, replica_groups=mesh['gx'=8,'xp'=2,'xl'=2,'zh'=2,'yp'=2,'yl'=2,'core'=2] {'xp','xl'}, dimensions={0}, use_global_device_ids=true | all-gather | bytes 983040 | tf_op jit(solution)/shard_map/all_gather | solution.py:232
  193.3 3.5 %close.1 = bf16[192,3072]{1,0:T(8,128)(2,1)} custom-call(f32[192,3072]{1,0:T(8,128)S(1)} %get-tuple-element.42.own, bf16[192,3072]{1,0:T(8,128)(2,1)} %collective-permute-done.17.passed), custom_call_target="tpu_custom_call" | custom-call | tf_op jit(solution)/shard_map/close/pallas_call | solution.py:250
  (47 shorter events, 10.9 us)
Async XLA Ops:
  0.6 1.1 copy-start.6
  1.8 22.2 %copy-start.7 = (bf16[192,3072]{1,0:T(8,128)(2,1)S(1)}, bf16[192,3072]{1,0:T(8,128)(2,1)}, u32[]{:S(2)}) copy-start(bf16[192,3072]{1,0:T(8,128)(2,1)} %refs_12_) | copy-start | bytes 3538948
  3.9 35.2 %all-to-all-start = ((bf16[32,16,192]{2,1,0:T(8,128)(2,1)}), bf16[32,16,192]{2,1,0:T(8,128)(2,1)S(1)}, u32[]{:S(2)}, u32[]{:S(2)}) async-start(bf16[32,16,192]{2,1,0:T(8,128)(2,1)} %part.1), calls=%async_computation | async-start | bytes 524288 | tf_op jit(solution)/shard_map/all_to_all | solution.py:176
  17.7 17.3 %collective-permute-start.1 = (bf16[32,3072]{1,0:T(8,128)(2,1)S(1)}, bf16[32,3072]{1,0:T(8,128)(2,1)S(1)}, u32[]{:S(2)}, u32[]{:S(2)}) collective-permute-start(bf16[32,3072]{1,0:T(8,128)(2,1)S(1)} %fusion.6.refs_0_), channel_id=1, source_target_pairs={{0,64},{128,0},{256,128},{384,256},{448,384},{320,448},{192,320},{... | collective-permute-start | bytes 589832 | tf_op jit(solution)/shard_map/ppermute | solution.py:28
  22.0 17.1 %collective-permute-start = (bf16[32,3072]{1,0:T(8,128)(2,1)S(1)}, bf16[32,3072]{1,0:T(8,128)(2,1)S(1)}, u32[]{:S(2)}, u32[]{:S(2)}) collective-permute-start(bf16[32,3072]{1,0:T(8,128)(2,1)S(1)} %fusion.6.refs_0_), channel_id=1, source_target_pairs={{0,128},{128,256},{256,384},{384,448},{448,320},{320,192},{192,64}... | collective-permute-start | bytes 589832 | tf_op jit(solution)/shard_map/ppermute | solution.py:28
  23.9 46.6 %collective-permute-start.2 = (bf16[192,3072]{1,0:T(8,128)(2,1)S(1)}, bf16[192,3072]{1,0:T(8,128)(2,1)S(1)}, u32[]{:S(2)}, u32[]{:S(2)}) collective-permute-start(bf16[192,3072]{1,0:T(8,128)(2,1)S(1)} %copy-done.7), channel_id=1, source_target_pairs={{0,2},{2,0},{1,3},{3,1},{4,6},{6,4},{5,7},{7,5},{8,10},{10,8},{9,1... | collective-permute-start | bytes 3538952 | tf_op jit(solution)/shard_map/ppermute | solution.py:32
  39.1 13.3 %collective-permute-start.3 = (bf16[32,3072]{1,0:T(8,128)(2,1)S(1)}, bf16[32,3072]{1,0:T(8,128)(2,1)S(1)}, u32[]{:S(2)}, u32[]{:S(2)}) collective-permute-start(bf16[32,3072]{1,0:T(8,128)(2,1)S(1)} %collective-permute-done.refs_1_), channel_id=1, source_target_pairs={{0,128},{128,256},{256,384},{384,448},{448,320},{320,192},{192,64}... | collective-permute-start | bytes 589832 | tf_op jit(solution)/shard_map/ppermute | solution.py:28
  41.0 17.5 %collective-permute-start.5 = (bf16[64,3072]{1,0:T(8,128)(2,1)S(1)}, bf16[64,3072]{1,0:T(8,128)(2,1)S(1)}, u32[]{:S(2)}, u32[]{:S(2)}) collective-permute-start(bf16[64,3072]{1,0:T(8,128)(2,1)S(1)} %pad_maximum_fusion.1), channel_id=1, source_target_pairs={{0,6},{2,4},{4,2},{6,0},{1,7},{3,5},{5,3},{7,1},{8,14},{10,12},{12... | collective-permute-start | bytes 1179656 | tf_op jit(solution)/shard_map/ppermute | solution.py:36
  45.8 12.8 %collective-permute-start.4 = (bf16[32,3072]{1,0:T(8,128)(2,1)S(1)}, bf16[32,3072]{1,0:T(8,128)(2,1)S(1)}, u32[]{:S(2)}, u32[]{:S(2)}) collective-permute-start(bf16[32,3072]{1,0:T(8,128)(2,1)S(1)} %collective-permute-done.1.refs_2_), channel_id=1, source_target_pairs={{0,64},{128,0},{256,128},{384,256},{448,384},{320,448},{192,320},{... | collective-permute-start | bytes 589832 | tf_op jit(solution)/shard_map/ppermute | solution.py:28
  52.5 22.7 %collective-permute-start.8 = (bf16[64,3072]{1,0:T(8,128)(2,1)S(1)}, bf16[64,3072]{1,0:T(8,128)(2,1)S(1)}, u32[]{:S(2)}, u32[]{:S(2)}) collective-permute-start(bf16[64,3072]{1,0:T(8,128)(2,1)S(1)} %pad_maximum_fusion.2), channel_id=1, source_target_pairs={{0,6},{2,4},{4,2},{6,0},{1,7},{3,5},{5,3},{7,1},{8,14},{10,12},{12... | collective-permute-start | bytes 1179656 | tf_op jit(solution)/shard_map/ppermute | solution.py:36
  55.2 17.3 %collective-permute-start.9 = (bf16[8,4,16,192]{3,2,1,0:T(8,128)(2,1)S(1)}, bf16[8,4,16,192]{3,2,1,0:T(8,128)(2,1)S(1)}, u32[]{:S(2)}, u32[]{:S(2)}) collective-permute-start(bf16[8,4,16,192]{3,2,1,0:T(8,128)(2,1)S(1)} %bitcast.8), channel_id=1, source_target_pairs={{0,16},{16,0},{1,17},{17,1},{2,18},{18,2},{3,19},{19,3},{4,20},{20... | collective-permute-start | bytes 589832 | tf_op jit(solution)/shard_map/ppermute | solution.py:32
  58.6 16.6 %collective-permute-start.6 = (bf16[32,3072]{1,0:T(8,128)(2,1)S(1)}, bf16[32,3072]{1,0:T(8,128)(2,1)S(1)}, u32[]{:S(2)}, u32[]{:S(2)}) collective-permute-start(bf16[32,3072]{1,0:T(8,128)(2,1)S(1)} %collective-permute-done.3.refs_3_), channel_id=1, source_target_pairs={{0,128},{128,256},{256,384},{384,448},{448,320},{320,192},{192,64}... | collective-permute-start | bytes 589832 | tf_op jit(solution)/shard_map/ppermute | solution.py:28
  62.9 12.3 %collective-permute-start.7 = (bf16[32,3072]{1,0:T(8,128)(2,1)S(1)}, bf16[32,3072]{1,0:T(8,128)(2,1)S(1)}, u32[]{:S(2)}, u32[]{:S(2)}) collective-permute-start(bf16[32,3072]{1,0:T(8,128)(2,1)S(1)} %collective-permute-done.4.refs_4_), channel_id=1, source_target_pairs={{0,64},{128,0},{256,128},{384,256},{448,384},{320,448},{192,320},{... | collective-permute-start | bytes 589832 | tf_op jit(solution)/shard_map/ppermute | solution.py:28
  70.5 17.6 %copy-start.8 = (bf16[192,3072]{1,0:T(8,128)(2,1)}, bf16[192,3072]{1,0:T(8,128)(2,1)S(1)}, u32[]{:S(2)}) copy-start(bf16[192,3072]{1,0:T(8,128)(2,1)S(1)} %collective-permute-done.2.refs_13_) | copy-start | bytes 3538948
  70.5 29.1 %collective-permute-start.13 = (bf16[192,3072]{1,0:T(8,128)(2,1)S(1)}, bf16[192,3072]{1,0:T(8,128)(2,1)S(1)}, u32[]{:S(2)}, u32[]{:S(2)}) collective-permute-start(bf16[192,3072]{1,0:T(8,128)(2,1)S(1)} %copy-done.7), channel_id=1, source_target_pairs={{0,1},{1,0},{2,3},{3,2},{4,5},{5,4},{6,7},{7,6},{8,9},{9,8},{10,11... | collective-permute-start | bytes 3538952 | tf_op jit(solution)/shard_map/ppermute | solution.py:32
  72.5 34.8 %copy-start.1 = (bf16[8,4,16,192]{3,2,1,0:T(8,128)(2,1)}, bf16[8,4,16,192]{3,2,1,0:T(8,128)(2,1)S(1)}, u32[]{:S(2)}) copy-start(bf16[8,4,16,192]{3,2,1,0:T(8,128)(2,1)S(1)} %collective-permute-done.9.refs_1_) | copy-start | bytes 589828
  72.5 27.2 %collective-permute-start.14 = (bf16[192,3072]{1,0:T(8,128)(2,1)S(1)}, bf16[192,3072]{1,0:T(8,128)(2,1)S(1)}, u32[]{:S(2)}, u32[]{:S(2)}) collective-permute-start(bf16[192,3072]{1,0:T(8,128)(2,1)S(1)} %collective-permute-done.2.refs_13_), channel_id=1, source_target_pairs={{0,1},{1,0},{2,3},{3,2},{4,5},{5,4},{6,7},{7,6},{8,9},{9,8},{10,11... | collective-permute-start | bytes 3538952 | tf_op jit(solution)/shard_map/ppermute | solution.py:32
  75.2 10.8 %collective-permute-start.10 = (bf16[32,3072]{1,0:T(8,128)(2,1)S(1)}, bf16[32,3072]{1,0:T(8,128)(2,1)S(1)}, u32[]{:S(2)}, u32[]{:S(2)}) collective-permute-start(bf16[32,3072]{1,0:T(8,128)(2,1)S(1)} %collective-permute-done.6.refs_5_), channel_id=1, source_target_pairs={{0,128},{128,256},{256,384},{384,448},{448,320},{320,192},{192,64}... | collective-permute-start | bytes 589832 | tf_op jit(solution)/shard_map/ppermute | solution.py:28
  77.1 15.6 %collective-permute-start.11 = (bf16[64,3072]{1,0:T(8,128)(2,1)S(1)}, bf16[64,3072]{1,0:T(8,128)(2,1)S(1)}, u32[]{:S(2)}, u32[]{:S(2)}) collective-permute-start(bf16[64,3072]{1,0:T(8,128)(2,1)S(1)} %pad_maximum_fusion.3), channel_id=1, source_target_pairs={{0,6},{2,4},{4,2},{6,0},{1,7},{3,5},{5,3},{7,1},{8,14},{10,12},{12... | collective-permute-start | bytes 1179656 | tf_op jit(solution)/shard_map/ppermute | solution.py:36
  86.1 13.6 %collective-permute-start.12 = (bf16[64,3072]{1,0:T(8,128)(2,1)S(1)}, bf16[64,3072]{1,0:T(8,128)(2,1)S(1)}, u32[]{:S(2)}, u32[]{:S(2)}) collective-permute-start(bf16[64,3072]{1,0:T(8,128)(2,1)S(1)} %pad_maximum_fusion.4), channel_id=1, source_target_pairs={{0,6},{2,4},{4,2},{6,0},{1,7},{3,5},{5,3},{7,1},{8,14},{10,12},{12... | collective-permute-start | bytes 1179656 | tf_op jit(solution)/shard_map/ppermute | solution.py:36
  88.1 19.1 %collective-permute-start.15 = (bf16[2,8,4,16,192]{4,3,2,1,0:T(8,128)(2,1)S(1)}, bf16[2,8,4,16,192]{4,3,2,1,0:T(8,128)(2,1)S(1)}, u32[]{:S(2)}, u32[]{:S(2)}) collective-permute-start(bf16[2,8,4,16,192]{4,3,2,1,0:T(8,128)(2,1)S(1)} %pad_maximum_fusion), channel_id=1, source_target_pairs={{0,32},{32,0},{1,33},{33,1},{2,34},{34,2},{3,35},{35,3},{4,36},{36... | collective-permute-start | bytes 1179656 | tf_op jit(solution)/shard_map/ppermute | solution.py:32
  99.7 1.0 copy-start.9
  100.7 1.1 copy-start.10
  107.2 5.6 %copy-start.3 = (bf16[2,8,4,16,192]{4,3,2,1,0:T(8,128)(2,1)}, bf16[2,8,4,16,192]{4,3,2,1,0:T(8,128)(2,1)S(1)}, u32[]{:S(2)}) copy-start(bf16[2,8,4,16,192]{4,3,2,1,0:T(8,128)(2,1)S(1)} %collective-permute-done.15.refs_2_) | copy-start | bytes 1179652
  112.8 39.7 %collective-permute-start.16 = (bf16[2,192,3072]{2,1,0:T(8,128)(2,1)}, bf16[2,192,3072]{2,1,0:T(8,128)(2,1)}, u32[]{:S(2)}, u32[]{:S(2)}) collective-permute-start(bf16[2,192,3072]{2,1,0:T(8,128)(2,1)} %weight_sums.3), channel_id=1, source_target_pairs={{0,1},{1,0},{2,3},{3,2},{4,5},{5,4},{6,7},{7,6},{8,9},{9,8},{10,11... | collective-permute-start | bytes 7077896 | tf_op jit(solution)/shard_map/ppermute | solution.py:32
  114.7 31.7 %copy-start = (bf16[512,3072]{1,0:T(8,128)(2,1)S(1)}, bf16[512,3072]{1,0:T(8,128)(2,1)}, u32[]{:S(2)}) copy-start(bf16[512,3072]{1,0:T(8,128)(2,1)} %get-tuple-element.41.refs_3_) | copy-start | bytes 9437188
  135.6 0.8 copy-start.5
  136.4 41.5 %all-to-all-start.2 = ((bf16[16,64,192]{2,1,0:T(8,128)(2,1)}), bf16[16,64,192]{2,1,0:T(8,128)(2,1)}, u32[]{:S(2)}, u32[]{:S(2)}) async-start(bf16[16,64,192]{2,1,0:T(8,128)(2,1)} %bitcast.15), calls=%async_computation.2 | async-start | bytes 1048576 | tf_op jit(solution)/shard_map/all_to_all | solution.py:228
  146.4 1.0 copy-start.2
  147.4 1.0 copy-start.4
  157.2 36.1 %collective-permute-start.17 = (bf16[192,3072]{1,0:T(8,128)(2,1)}, bf16[192,3072]{1,0:T(8,128)(2,1)}, u32[]{:S(2)}, u32[]{:S(2)}) collective-permute-start(bf16[192,3072]{1,0:T(8,128)(2,1)} %get-tuple-element.43), channel_id=1, source_target_pairs={{0,2},{2,0},{1,3},{3,1},{4,6},{6,4},{5,7},{7,5},{8,10},{10,8},{9,1... | collective-permute-start | bytes 3538952 | tf_op jit(solution)/shard_map/ppermute | solution.py:32

commit v4 on v3

--- a/solution.py
+++ b/solution.py
@@ -133,7 +133,9 @@
 
 def pair_kernel(parts, out):
     sums = [parts[k, 0].astype(F32) + parts[k, 1].astype(F32) for k in range(8)]
-    out[...] = jnp.concatenate(sums, 1).astype(BF16)
+    total = jnp.concatenate(sums, 1).astype(BF16)
+    for x in range(4):
+        out[x] = total
 
 
 def place_kernel(parts, out):
@@ -181,15 +183,11 @@
         up.append(hop(up[-1], 1))
         far.append(across(jnp.concatenate([down[-1], up[-1]], 0)))
         down.append(hop(down[-1], -1))
-        if s == 0:
-            up[1], down[1], part = lax.optimization_barrier((up[1], down[1], part))
-            beside_x = swap(part, "xl")
         if s == 1:
             up[2], down[2], far[0] = lax.optimization_barrier((up[2], down[2], far[0]))
         if s == 2:
-            up[3], down[3], far[1], beside_x = lax.optimization_barrier(
-                (up[3], down[3], far[1], beside_x)
-            )
+            up[3], down[3], far[1], part = lax.optimization_barrier((up[3], down[3], far[1], part))
+            beside_x = swap(part, "xl")
             cols = (part, beside_x, swap(jnp.stack([part, beside_x], 0), "xp"))
     up.append(hop(up[3], 1))
     far.append(across(jnp.concatenate([down[3], up[4]], 0)))
@@ -228,8 +226,8 @@
     rows = lax.all_to_all(
         rows.reshape(16, 64, 192), ("gx", "zh"), split_axis=0, concat_axis=0, tiled=True
     )
-    rows = whole_call(pair_kernel, (64, 1536), "sum_z")(rows.reshape(8, 2, 64, 192))
-    rows = lax.all_gather(rows, ("xp", "xl"), axis=0)
+    rows = whole_call(pair_kernel, (4, 64, 1536), "sum_z")(rows.reshape(8, 2, 64, 192))
+    rows = lax.all_to_all(rows, ("xp", "xl"), split_axis=0, concat_axis=0, tiled=True)
     grad_in = whole_call(place_kernel, (256, 1536), "place")(rows.reshape(4, 4, 16, 1536))
 
     met = swap(send, "core")

time: 198 us -> 190 us (0.960)
  waiting for transfers between devices: 43.4 us -> 30.5 us
  starting transfers between devices: 84.6 us -> 90.9 us
  local copies, waits for them, and re-layouts: 6.02 us -> 3.91 us
    all_gather x1 -> x0, blocking collectives: 13.3 us -> none  [shards(): rows = lax.all_gather(rows, ('xp', 'xl'), axis=0)]
    ppermute x7, waiting for transfers between devices: 18 us -> 5.32 us  [hop(): lax.ppermute(value, 'gx', [(RING[q], RING[(q + step) % 8]) for q in range...]
    all_to_all x0 -> x1, blocking collectives: none -> 12.4 us  [shards(): lax.all_to_all(rows, ('xp', 'xl'), split_axis=0, concat_axis=0, tiled=True)]
    ppermute x7, starting transfers between devices: 28.5 us -> 34.5 us  [hop(): lax.ppermute(value, 'gx', [(RING[q], RING[(q + step) % 8]) for q in range...]
    ppermute x4, starting transfers between devices: 12.3 us -> 17 us  [across(): return lax.ppermute(value, ('yp', 'yl'), [(k, 3 - k) for k in range(4)])]
    all_to_all x1, starting transfers between devices: 13.8 us -> 10.9 us  [shards(): lax.all_to_all(part, ('gx', 'yl', 'core'), split_axis=0, concat_axis=0, t...]
    unnamed x22 -> x16, local copies, waits for them, and re-layouts: 6.02 us -> 3.91 us
  transfers between devices with their start and end apart: 20 -> 20, of which waited for: 6 -> 5; matrix products, arithmetic and copies ran while one was open for 0% -> 1% of each run, Pallas kernels for 8% -> 9%
where the time goes in v4:
time: 190 us; the launch traced here: 189 us
  starting transfers between devices  90.9 us (48%)
  blocking collectives  33.4 us (18%)
  waiting for transfers between devices  30.5 us (16%)
  Pallas kernels  26.5 us (14%)
  local copies, waits for them, and re-layouts  3.91 us (2%)
  other arithmetic  2.25 us (1%)
    ppermute x7, starting transfers between devices, hop(): lax.ppermute(value, 'gx', [(RING[q], RING[(q + step) % 8]) for q in range...  34.5 us
    all_to_all x1, blocking collectives, shards(): lax.all_to_all(rows.reshape(16, 8, 16, 192), ('xp', 'xl', 'yl', 'core'),...  21 us
    ppermute x7, starting transfers between devices, swap(): return lax.ppermute(value, axis, [(0, 1), (1, 0)])  18.8 us
    all_to_all x1, waiting for transfers between devices, shards(): lax.all_to_all(rows.reshape(16, 64, 192), ('gx', 'zh'), split_axis=0, con...  18.5 us
    ppermute x4, starting transfers between devices, across(): return lax.ppermute(value, ('yp', 'yl'), [(k, 3 - k) for k in range(4)])  17 us
    all_to_all x1, blocking collectives, shards(): lax.all_to_all(rows, ('xp', 'xl'), split_axis=0, concat_axis=0, tiled=True)  12.4 us
    all_to_all x1, starting transfers between devices, shards(): lax.all_to_all(part, ('gx', 'yl', 'core'), split_axis=0, concat_axis=0, t...  10.9 us
    all_to_all x1, starting transfers between devices, shards(): lax.all_to_all(rows.reshape(16, 64, 192), ('gx', 'zh'), split_axis=0, con...  9.79 us
  transfers between devices with their start and end apart: 20, of which 5 were waited for; matrix products, arithmetic and copies ran while one was open for 1% of the time, Pallas kernels for 9%

profile of v4, /device:TPU:32, one launch (start us, length us, event | category | flops | bytes accessed | tf_op | source)
XLA Modules:
  0.0 188.5 jit_solution(13011593795021323224)
XLA Ops:
  2.6 1.3 fusion.6.refs_0_
  3.9 7.4 %collective-permute-start = (bf16[32,3072]{1,0:T(8,128)(2,1)S(1)}, bf16[32,3072]{1,0:T(8,128)(2,1)S(1)}, u32[]{:S(2)}, u32[]{:S(2)}) collective-permute-start(bf16[32,3072]{1,0:T(8,128)(2,1)S(1)} %fusion.6.refs_0_), channel_id=1, source_target_pairs={{0,128},{128,256},{256,384},{384,448},{448,320},{320,192},{192,64}... | collective-permute-start | bytes 589832 | tf_op jit(solution)/shard_map/ppermute | solution.py:28
  11.3 1.9 %collective-permute-start.2 = (bf16[192,3072]{1,0:T(8,128)(2,1)S(1)}, bf16[192,3072]{1,0:T(8,128)(2,1)}, u32[]{:S(2)}, u32[]{:S(2)}) collective-permute-start(bf16[192,3072]{1,0:T(8,128)(2,1)S(1)} %copy-done.7), channel_id=1, source_target_pairs={{0,2},{2,0},{1,3},{3,1},{4,6},{6,4},{5,7},{7,5},{8,10},{10,8},{9,1... | collective-permute-start | bytes 3538952 | tf_op jit(solution)/shard_map/ppermute | solution.py:32
  13.2 1.9 %collective-permute-start.1 = (bf16[32,3072]{1,0:T(8,128)(2,1)S(1)}, bf16[32,3072]{1,0:T(8,128)(2,1)S(1)}, u32[]{:S(2)}, u32[]{:S(2)}) collective-permute-start(bf16[32,3072]{1,0:T(8,128)(2,1)S(1)} %fusion.6.refs_0_), channel_id=1, source_target_pairs={{0,64},{128,0},{256,128},{384,256},{448,384},{320,448},{192,320},{... | collective-permute-start | bytes 589832 | tf_op jit(solution)/shard_map/ppermute | solution.py:28
  15.2 10.9 %all-to-all-start = ((bf16[32,16,192]{2,1,0:T(8,128)(2,1)}), bf16[32,16,192]{2,1,0:T(8,128)(2,1)S(1)}, u32[]{:S(2)}, u32[]{:S(2)}) async-start(bf16[32,16,192]{2,1,0:T(8,128)(2,1)} %part.1), calls=%async_computation | async-start | bytes 524288 | tf_op jit(solution)/shard_map/all_to_all | solution.py:178
  26.1 2.1 %collective-permute-start.3 = (bf16[32,3072]{1,0:T(8,128)(2,1)S(1)}, bf16[32,3072]{1,0:T(8,128)(2,1)S(1)}, u32[]{:S(2)}, u32[]{:S(2)}) collective-permute-start(bf16[32,3072]{1,0:T(8,128)(2,1)S(1)} %collective-permute-done.refs_1_), channel_id=1, source_target_pairs={{0,128},{128,256},{256,384},{384,448},{448,320},{320,192},{192,64}... | collective-permute-start | bytes 589832 | tf_op jit(solution)/shard_map/ppermute | solution.py:28
  28.3 5.3 %collective-permute-start.5 = (bf16[64,3072]{1,0:T(8,128)(2,1)S(1)}, bf16[64,3072]{1,0:T(8,128)(2,1)S(1)}, u32[]{:S(2)}, u32[]{:S(2)}) collective-permute-start(bf16[64,3072]{1,0:T(8,128)(2,1)S(1)} %pad_maximum_fusion.1), channel_id=1, source_target_pairs={{0,6},{2,4},{4,2},{6,0},{1,7},{3,5},{5,3},{7,1},{8,14},{10,12},{12... | collective-permute-start | bytes 1179656 | tf_op jit(solution)/shard_map/ppermute | solution.py:36
  33.6 4.3 %collective-permute-start.4 = (bf16[32,3072]{1,0:T(8,128)(2,1)S(1)}, bf16[32,3072]{1,0:T(8,128)(2,1)S(1)}, u32[]{:S(2)}, u32[]{:S(2)}) collective-permute-start(bf16[32,3072]{1,0:T(8,128)(2,1)S(1)} %collective-permute-done.1.refs_2_), channel_id=1, source_target_pairs={{0,64},{128,0},{256,128},{384,256},{448,384},{320,448},{192,320},{... | collective-permute-start | bytes 589832 | tf_op jit(solution)/shard_map/ppermute | solution.py:28
  37.9 4.9 %collective-permute-done.3.refs_3_ = bf16[32,3072]{1,0:T(8,128)(2,1)S(1)} collective-permute-done((bf16[32,3072]{1,0:T(8,128)(2,1)S(1)}, bf16[32,3072]{1,0:T(8,128)(2,1)S(1)}, u32[]{:S(2)}, u32[]{:S(2)}) %collective-permute-start.3) | collective-permute-done | bytes 196640 | tf_op jit(solution)/shard_map/ppermute | solution.py:28
  43.5 5.0 %collective-permute-start.8 = (bf16[64,3072]{1,0:T(8,128)(2,1)}, bf16[64,3072]{1,0:T(8,128)(2,1)}, u32[]{:S(2)}, u32[]{:S(2)}) collective-permute-start(bf16[64,3072]{1,0:T(8,128)(2,1)} %pad_maximum_fusion.2), channel_id=1, source_target_pairs={{0,6},{2,4},{4,2},{6,0},{1,7},{3,5},{5,3},{7,1},{8,14},{10,12},{12... | collective-permute-start | bytes 1179656 | tf_op jit(solution)/shard_map/ppermute | solution.py:36
  48.6 2.6 %collective-permute-start.6 = (bf16[32,3072]{1,0:T(8,128)(2,1)S(1)}, bf16[32,3072]{1,0:T(8,128)(2,1)S(1)}, u32[]{:S(2)}, u32[]{:S(2)}) collective-permute-start(bf16[32,3072]{1,0:T(8,128)(2,1)S(1)} %collective-permute-done.3.refs_3_), channel_id=1, source_target_pairs={{0,128},{128,256},{256,384},{384,448},{448,320},{320,192},{192,64}... | collective-permute-start | bytes 589832 | tf_op jit(solution)/shard_map/ppermute | solution.py:28
  51.2 10.5 %collective-permute-start.7 = (bf16[32,3072]{1,0:T(8,128)(2,1)S(1)}, bf16[32,3072]{1,0:T(8,128)(2,1)S(1)}, u32[]{:S(2)}, u32[]{:S(2)}) collective-permute-start(bf16[32,3072]{1,0:T(8,128)(2,1)S(1)} %collective-permute-done.4.refs_4_), channel_id=1, source_target_pairs={{0,64},{128,0},{256,128},{384,256},{448,384},{320,448},{192,320},{... | collective-permute-start | bytes 589832 | tf_op jit(solution)/shard_map/ppermute | solution.py:28
  61.7 1.9 %collective-permute-start.12 = (bf16[192,3072]{1,0:T(8,128)(2,1)S(1)}, bf16[192,3072]{1,0:T(8,128)(2,1)}, u32[]{:S(2)}, u32[]{:S(2)}) collective-permute-start(bf16[192,3072]{1,0:T(8,128)(2,1)S(1)} %copy-done.7), channel_id=1, source_target_pairs={{0,1},{1,0},{2,3},{3,2},{4,5},{5,4},{6,7},{7,6},{8,9},{9,8},{10,11... | collective-permute-start | bytes 3538952 | tf_op jit(solution)/shard_map/ppermute | solution.py:32
  63.6 2.4 %collective-permute-start.13 = (bf16[192,3072]{1,0:T(8,128)(2,1)}, bf16[192,3072]{1,0:T(8,128)(2,1)}, u32[]{:S(2)}, u32[]{:S(2)}) collective-permute-start(bf16[192,3072]{1,0:T(8,128)(2,1)} %collective-permute-done.2.refs_13_), channel_id=1, source_target_pairs={{0,1},{1,0},{2,3},{3,2},{4,5},{5,4},{6,7},{7,6},{8,9},{9,8},{10,11... | collective-permute-start | bytes 3538952 | tf_op jit(solution)/shard_map/ppermute | solution.py:32
  66.1 5.7 %collective-permute-start.9 = (bf16[32,3072]{1,0:T(8,128)(2,1)S(1)}, bf16[32,3072]{1,0:T(8,128)(2,1)S(1)}, u32[]{:S(2)}, u32[]{:S(2)}) collective-permute-start(bf16[32,3072]{1,0:T(8,128)(2,1)S(1)} %collective-permute-done.6.refs_5_), channel_id=1, source_target_pairs={{0,128},{128,256},{256,384},{384,448},{448,320},{320,192},{192,64}... | collective-permute-start | bytes 589832 | tf_op jit(solution)/shard_map/ppermute | solution.py:28
  71.8 2.2 %collective-permute-start.10 = (bf16[64,3072]{1,0:T(8,128)(2,1)S(1)}, bf16[64,3072]{1,0:T(8,128)(2,1)S(1)}, u32[]{:S(2)}, u32[]{:S(2)}) collective-permute-start(bf16[64,3072]{1,0:T(8,128)(2,1)S(1)} %pad_maximum_fusion.3), channel_id=1, source_target_pairs={{0,6},{2,4},{4,2},{6,0},{1,7},{3,5},{5,3},{7,1},{8,14},{10,12},{12... | collective-permute-start | bytes 1179656 | tf_op jit(solution)/shard_map/ppermute | solution.py:36
  74.0 3.4 %collective-permute-start.14 = (bf16[8,4,16,192]{3,2,1,0:T(8,128)(2,1)S(1)}, bf16[8,4,16,192]{3,2,1,0:T(8,128)(2,1)S(1)}, u32[]{:S(2)}, u32[]{:S(2)}) collective-permute-start(bf16[8,4,16,192]{3,2,1,0:T(8,128)(2,1)S(1)} %bitcast.8), channel_id=1, source_target_pairs={{0,16},{16,0},{1,17},{17,1},{2,18},{18,2},{3,19},{19,3},{4,20},{20... | collective-permute-start | bytes 589832 | tf_op jit(solution)/shard_map/ppermute | solution.py:32
  77.9 4.5 %collective-permute-start.11 = (bf16[64,3072]{1,0:T(8,128)(2,1)S(1)}, bf16[64,3072]{1,0:T(8,128)(2,1)S(1)}, u32[]{:S(2)}, u32[]{:S(2)}) collective-permute-start(bf16[64,3072]{1,0:T(8,128)(2,1)S(1)} %pad_maximum_fusion.4), channel_id=1, source_target_pairs={{0,6},{2,4},{4,2},{6,0},{1,7},{3,5},{5,3},{7,1},{8,14},{10,12},{12... | collective-permute-start | bytes 1179656 | tf_op jit(solution)/shard_map/ppermute | solution.py:36
  82.3 1.2 collective-permute-done.14.refs_1_
  83.7 4.9 %collective-permute-start.15 = (bf16[2,8,4,16,192]{4,3,2,1,0:T(8,128)(2,1)S(1)}, bf16[2,8,4,16,192]{4,3,2,1,0:T(8,128)(2,1)S(1)}, u32[]{:S(2)}, u32[]{:S(2)}) collective-permute-start(bf16[2,8,4,16,192]{4,3,2,1,0:T(8,128)(2,1)S(1)} %pad_maximum_fusion), channel_id=1, source_target_pairs={{0,32},{32,0},{1,33},{33,1},{2,34},{34,2},{3,35},{35,3},{4,36},{36... | collective-permute-start | bytes 1179656 | tf_op jit(solution)/shard_map/ppermute | solution.py:32
  88.6 5.5 %collective-permute-done.11.refs_11_ = bf16[64,3072]{1,0:T(8,128)(2,1)S(1)} collective-permute-done((bf16[64,3072]{1,0:T(8,128)(2,1)S(1)}, bf16[64,3072]{1,0:T(8,128)(2,1)S(1)}, u32[]{:S(2)}, u32[]{:S(2)}) %collective-permute-start.11) | collective-permute-done | bytes 393248 | tf_op jit(solution)/shard_map/ppermute | solution.py:36
  94.1 5.6 %products.1 = (bf16[4,4,8,16,192]{4,3,2,1,0:T(8,128)(2,1)S(1)}, bf16[512,3072]{1,0:T(8,128)(2,1)}) custom-call(bf16[32,3072]{1,0:T(8,128)(2,1)S(1)} %fusion.6.refs_0_, bf16[32,3072]{1,0:T(8,128)(2,1)S(1)} %collective-permute-done.refs_1_, bf16[32,3072]{1,0:T(8,128)(2,1)S(1)} %collective-permute-done.1.refs_2_, ...), custom_call_target="tpu_custom_call" | custom-call | flops 2415919104 | bytes 12582912 | tf_op jit(solution)/shard_map/products/pallas_call | solution.py:199
  99.7 5.6 %weight_sums.3 = bf16[2,192,3072]{2,1,0:T(8,128)(2,1)} custom-call(bf16[8,4,16,192]{3,2,1,0:T(8,128)(2,1)S(1)} %bitcast.10, bf16[8,4,16,192]{3,2,1,0:T(8,128)(2,1)S(1)} %collective-permute-done.14.refs_1_, bf16[2,8,4,16,192]{4,3,2,1,0:T(8,128)(2,1)S(1)} %collective-permute-done.15.refs_2_, bf16[512,3072]{1,0:T(8,128)(2,1)} %get-tuple-element.35.refs_3_), custom_call_target="tpu_custom_call" | custom-call | flops 1207959552 | bytes 8388608 | tf_op jit(solution)/shard_map/weight_sums/pallas_call | solution.py:107
  105.2 1.9 %collective-permute-start.16 = (bf16[2,192,3072]{2,1,0:T(8,128)(2,1)}, bf16[2,192,3072]{2,1,0:T(8,128)(2,1)}, u32[]{:S(2)}, u32[]{:S(2)}) collective-permute-start(bf16[2,192,3072]{2,1,0:T(8,128)(2,1)} %weight_sums.3), channel_id=1, source_target_pairs={{0,1},{1,0},{2,3},{3,2},{4,5},{5,4},{6,7},{7,6},{8,9},{9,8},{10,11... | collective-permute-start | bytes 7077896 | tf_op jit(solution)/shard_map/ppermute | solution.py:32
  107.2 21.0 %all_to_all.20 = bf16[16,8,16,192]{3,2,1,0:T(8,128)(2,1)S(1)} all-to-all(bf16[16,8,16,192]{3,2,1,0:T(8,128)(2,1)S(1)} %bitcast.16), channel_id=1, replica_groups=mesh['gx'=8,'xp'=2,'xl'=2,'zh'=2,'yp'=2,'yl'=2,'core'=2] {'xp','xl','yl'..., dimensions={0} | all-to-all | bytes 1572864 | tf_op jit(solution)/shard_map/all_to_all | solution.py:216
  129.2 9.8 %all-to-all-start.2 = ((bf16[16,64,192]{2,1,0:T(8,128)(2,1)}), bf16[16,64,192]{2,1,0:T(8,128)(2,1)}, u32[]{:S(2)}, u32[]{:S(2)}) async-start(bf16[16,64,192]{2,1,0:T(8,128)(2,1)} %bitcast.15), calls=%async_computation.2 | async-start | bytes 1048576 | tf_op jit(solution)/shard_map/all_to_all | solution.py:226
  140.9 4.1 %weight_sums.2.keep = f32[2,192,3072]{2,1,0:T(8,128)} custom-call(bf16[8,4,16,192]{3,2,1,0:T(8,128)(2,1)S(1)} %bitcast.11, bf16[8,4,16,192]{3,2,1,0:T(8,128)(2,1)S(1)} %copy-done.2, bf16[2,8,4,16,192]{4,3,2,1,0:T(8,128)(2,1)S(1)} %copy-done.4, bf16[512,3072]{1,0:T(8,128)(2,1)S(1)} %copy-done), custom_call_target="tpu_custom_call" | custom-call | flops 1207959552 | bytes 8388608 | tf_op jit(solution)/shard_map/weight_sums/pallas_call | solution.py:107
  145.0 4.7 %meet.1 = (f32[192,3072]{1,0:T(8,128)S(1)}, bf16[192,3072]{1,0:T(8,128)(2,1)}) custom-call(f32[2,192,3072]{2,1,0:T(8,128)} %weight_sums.2.keep, bf16[2,192,3072]{2,1,0:T(8,128)(2,1)} %collective-permute-done.16.met), custom_call_target="tpu_custom_call" | custom-call | tf_op jit(solution)/shard_map/meet/pallas_call | solution.py:236
  149.7 2.3 %collective-permute-start.17 = (bf16[192,3072]{1,0:T(8,128)(2,1)}, bf16[192,3072]{1,0:T(8,128)(2,1)}, u32[]{:S(2)}, u32[]{:S(2)}) collective-permute-start(bf16[192,3072]{1,0:T(8,128)(2,1)} %get-tuple-element.37), channel_id=1, source_target_pairs={{0,2},{2,0},{1,3},{3,1},{4,6},{6,4},{5,7},{7,5},{8,10},{10,8},{9,1... | collective-permute-start | bytes 3538952 | tf_op jit(solution)/shard_map/ppermute | solution.py:32
  152.0 18.5 %all-to-all-done.2 = bf16[16,64,192]{2,1,0:T(8,128)(2,1)} async-done(((bf16[16,64,192]{2,1,0:T(8,128)(2,1)}), bf16[16,64,192]{2,1,0:T(8,128)(2,1)}, u32[]{:S(2)}, u32[]{:S(2)}) %all-to-all-start.2) | async-done | bytes 393248 | tf_op jit(solution)/shard_map/all_to_all | solution.py:226
  171.6 12.4 %all_to_all.21 = bf16[4,64,1536]{2,1,0:T(8,128)(2,1)S(1)} all-to-all(bf16[4,64,1536]{2,1,0:T(8,128)(2,1)S(1)} %sum_z.1), channel_id=1, replica_groups=mesh['gx'=8,'xp'=2,'xl'=2,'zh'=2,'yp'=2,'yl'=2,'core'=2] {'xp','xl'}, dimensions={0} | all-to-all | bytes 1572864 | tf_op jit(solution)/shard_map/all_to_all | solution.py:230
  185.0 3.5 %close.1 = bf16[192,3072]{1,0:T(8,128)(2,1)} custom-call(f32[192,3072]{1,0:T(8,128)S(1)} %get-tuple-element.36.own, bf16[192,3072]{1,0:T(8,128)(2,1)} %collective-permute-done.17.passed), custom_call_target="tpu_custom_call" | custom-call | tf_op jit(solution)/shard_map/close/pallas_call | solution.py:248
  (41 shorter events, 8.4 us)
Async XLA Ops:
  0.6 1.1 copy-start.6
  1.8 9.5 %copy-start.7 = (bf16[192,3072]{1,0:T(8,128)(2,1)S(1)}, bf16[192,3072]{1,0:T(8,128)(2,1)}, u32[]{:S(2)}) copy-start(bf16[192,3072]{1,0:T(8,128)(2,1)} %refs_12_) | copy-start | bytes 3538948
  3.9 22.2 %collective-permute-start = (bf16[32,3072]{1,0:T(8,128)(2,1)S(1)}, bf16[32,3072]{1,0:T(8,128)(2,1)S(1)}, u32[]{:S(2)}, u32[]{:S(2)}) collective-permute-start(bf16[32,3072]{1,0:T(8,128)(2,1)S(1)} %fusion.6.refs_0_), channel_id=1, source_target_pairs={{0,128},{128,256},{256,384},{384,448},{448,320},{320,192},{192,64}... | collective-permute-start | bytes 589832 | tf_op jit(solution)/shard_map/ppermute | solution.py:28
  11.3 50.4 %collective-permute-start.2 = (bf16[192,3072]{1,0:T(8,128)(2,1)S(1)}, bf16[192,3072]{1,0:T(8,128)(2,1)}, u32[]{:S(2)}, u32[]{:S(2)}) collective-permute-start(bf16[192,3072]{1,0:T(8,128)(2,1)S(1)} %copy-done.7), channel_id=1, source_target_pairs={{0,2},{2,0},{1,3},{3,1},{4,6},{6,4},{5,7},{7,5},{8,10},{10,8},{9,1... | collective-permute-start | bytes 3538952 | tf_op jit(solution)/shard_map/ppermute | solution.py:32
  13.2 20.4 %collective-permute-start.1 = (bf16[32,3072]{1,0:T(8,128)(2,1)S(1)}, bf16[32,3072]{1,0:T(8,128)(2,1)S(1)}, u32[]{:S(2)}, u32[]{:S(2)}) collective-permute-start(bf16[32,3072]{1,0:T(8,128)(2,1)S(1)} %fusion.6.refs_0_), channel_id=1, source_target_pairs={{0,64},{128,0},{256,128},{384,256},{448,384},{320,448},{192,320},{... | collective-permute-start | bytes 589832 | tf_op jit(solution)/shard_map/ppermute | solution.py:28
  15.2 50.9 %all-to-all-start = ((bf16[32,16,192]{2,1,0:T(8,128)(2,1)}), bf16[32,16,192]{2,1,0:T(8,128)(2,1)S(1)}, u32[]{:S(2)}, u32[]{:S(2)}) async-start(bf16[32,16,192]{2,1,0:T(8,128)(2,1)} %part.1), calls=%async_computation | async-start | bytes 524288 | tf_op jit(solution)/shard_map/all_to_all | solution.py:178
  26.1 16.7 %collective-permute-start.3 = (bf16[32,3072]{1,0:T(8,128)(2,1)S(1)}, bf16[32,3072]{1,0:T(8,128)(2,1)S(1)}, u32[]{:S(2)}, u32[]{:S(2)}) collective-permute-start(bf16[32,3072]{1,0:T(8,128)(2,1)S(1)} %collective-permute-done.refs_1_), channel_id=1, source_target_pairs={{0,128},{128,256},{256,384},{384,448},{448,320},{320,192},{192,64}... | collective-permute-start | bytes 589832 | tf_op jit(solution)/shard_map/ppermute | solution.py:28
  28.3 20.3 %collective-permute-start.5 = (bf16[64,3072]{1,0:T(8,128)(2,1)S(1)}, bf16[64,3072]{1,0:T(8,128)(2,1)S(1)}, u32[]{:S(2)}, u32[]{:S(2)}) collective-permute-start(bf16[64,3072]{1,0:T(8,128)(2,1)S(1)} %pad_maximum_fusion.1), channel_id=1, source_target_pairs={{0,6},{2,4},{4,2},{6,0},{1,7},{3,5},{5,3},{7,1},{8,14},{10,12},{12... | collective-permute-start | bytes 1179656 | tf_op jit(solution)/shard_map/ppermute | solution.py:36
  33.6 14.9 %collective-permute-start.4 = (bf16[32,3072]{1,0:T(8,128)(2,1)S(1)}, bf16[32,3072]{1,0:T(8,128)(2,1)S(1)}, u32[]{:S(2)}, u32[]{:S(2)}) collective-permute-start(bf16[32,3072]{1,0:T(8,128)(2,1)S(1)} %collective-permute-done.1.refs_2_), channel_id=1, source_target_pairs={{0,64},{128,0},{256,128},{384,256},{448,384},{320,448},{192,320},{... | collective-permute-start | bytes 589832 | tf_op jit(solution)/shard_map/ppermute | solution.py:28
  43.5 22.6 %collective-permute-start.8 = (bf16[64,3072]{1,0:T(8,128)(2,1)}, bf16[64,3072]{1,0:T(8,128)(2,1)}, u32[]{:S(2)}, u32[]{:S(2)}) collective-permute-start(bf16[64,3072]{1,0:T(8,128)(2,1)} %pad_maximum_fusion.2), channel_id=1, source_target_pairs={{0,6},{2,4},{4,2},{6,0},{1,7},{3,5},{5,3},{7,1},{8,14},{10,12},{12... | collective-permute-start | bytes 1179656 | tf_op jit(solution)/shard_map/ppermute | solution.py:36
  48.6 17.5 %collective-permute-start.6 = (bf16[32,3072]{1,0:T(8,128)(2,1)S(1)}, bf16[32,3072]{1,0:T(8,128)(2,1)S(1)}, u32[]{:S(2)}, u32[]{:S(2)}) collective-permute-start(bf16[32,3072]{1,0:T(8,128)(2,1)S(1)} %collective-permute-done.3.refs_3_), channel_id=1, source_target_pairs={{0,128},{128,256},{256,384},{384,448},{448,320},{320,192},{192,64}... | collective-permute-start | bytes 589832 | tf_op jit(solution)/shard_map/ppermute | solution.py:28
  51.2 14.9 %collective-permute-start.7 = (bf16[32,3072]{1,0:T(8,128)(2,1)S(1)}, bf16[32,3072]{1,0:T(8,128)(2,1)S(1)}, u32[]{:S(2)}, u32[]{:S(2)}) collective-permute-start(bf16[32,3072]{1,0:T(8,128)(2,1)S(1)} %collective-permute-done.4.refs_4_), channel_id=1, source_target_pairs={{0,64},{128,0},{256,128},{384,256},{448,384},{320,448},{192,320},{... | collective-permute-start | bytes 589832 | tf_op jit(solution)/shard_map/ppermute | solution.py:28
  61.7 32.4 %collective-permute-start.12 = (bf16[192,3072]{1,0:T(8,128)(2,1)S(1)}, bf16[192,3072]{1,0:T(8,128)(2,1)}, u32[]{:S(2)}, u32[]{:S(2)}) collective-permute-start(bf16[192,3072]{1,0:T(8,128)(2,1)S(1)} %copy-done.7), channel_id=1, source_target_pairs={{0,1},{1,0},{2,3},{3,2},{4,5},{5,4},{6,7},{7,6},{8,9},{9,8},{10,11... | collective-permute-start | bytes 3538952 | tf_op jit(solution)/shard_map/ppermute | solution.py:32
  63.6 30.5 %collective-permute-start.13 = (bf16[192,3072]{1,0:T(8,128)(2,1)}, bf16[192,3072]{1,0:T(8,128)(2,1)}, u32[]{:S(2)}, u32[]{:S(2)}) collective-permute-start(bf16[192,3072]{1,0:T(8,128)(2,1)} %collective-permute-done.2.refs_13_), channel_id=1, source_target_pairs={{0,1},{1,0},{2,3},{3,2},{4,5},{5,4},{6,7},{7,6},{8,9},{9,8},{10,11... | collective-permute-start | bytes 3538952 | tf_op jit(solution)/shard_map/ppermute | solution.py:32
  66.1 11.7 %collective-permute-start.9 = (bf16[32,3072]{1,0:T(8,128)(2,1)S(1)}, bf16[32,3072]{1,0:T(8,128)(2,1)S(1)}, u32[]{:S(2)}, u32[]{:S(2)}) collective-permute-start(bf16[32,3072]{1,0:T(8,128)(2,1)S(1)} %collective-permute-done.6.refs_5_), channel_id=1, source_target_pairs={{0,128},{128,256},{256,384},{384,448},{448,320},{320,192},{192,64}... | collective-permute-start | bytes 589832 | tf_op jit(solution)/shard_map/ppermute | solution.py:28
  71.8 16.8 %collective-permute-start.10 = (bf16[64,3072]{1,0:T(8,128)(2,1)S(1)}, bf16[64,3072]{1,0:T(8,128)(2,1)S(1)}, u32[]{:S(2)}, u32[]{:S(2)}) collective-permute-start(bf16[64,3072]{1,0:T(8,128)(2,1)S(1)} %pad_maximum_fusion.3), channel_id=1, source_target_pairs={{0,6},{2,4},{4,2},{6,0},{1,7},{3,5},{5,3},{7,1},{8,14},{10,12},{12... | collective-permute-start | bytes 1179656 | tf_op jit(solution)/shard_map/ppermute | solution.py:36
  74.0 9.6 %collective-permute-start.14 = (bf16[8,4,16,192]{3,2,1,0:T(8,128)(2,1)S(1)}, bf16[8,4,16,192]{3,2,1,0:T(8,128)(2,1)S(1)}, u32[]{:S(2)}, u32[]{:S(2)}) collective-permute-start(bf16[8,4,16,192]{3,2,1,0:T(8,128)(2,1)S(1)} %bitcast.8), channel_id=1, source_target_pairs={{0,16},{16,0},{1,17},{17,1},{2,18},{18,2},{3,19},{19,3},{4,20},{20... | collective-permute-start | bytes 589832 | tf_op jit(solution)/shard_map/ppermute | solution.py:32
  77.9 16.2 %collective-permute-start.11 = (bf16[64,3072]{1,0:T(8,128)(2,1)S(1)}, bf16[64,3072]{1,0:T(8,128)(2,1)S(1)}, u32[]{:S(2)}, u32[]{:S(2)}) collective-permute-start(bf16[64,3072]{1,0:T(8,128)(2,1)S(1)} %pad_maximum_fusion.4), channel_id=1, source_target_pairs={{0,6},{2,4},{4,2},{6,0},{1,7},{3,5},{5,3},{7,1},{8,14},{10,12},{12... | collective-permute-start | bytes 1179656 | tf_op jit(solution)/shard_map/ppermute | solution.py:36
  83.6 16.1 %copy-start.1 = (bf16[8,4,16,192]{3,2,1,0:T(8,128)(2,1)}, bf16[8,4,16,192]{3,2,1,0:T(8,128)(2,1)S(1)}, u32[]{:S(2)}) copy-start(bf16[8,4,16,192]{3,2,1,0:T(8,128)(2,1)S(1)} %collective-permute-done.14.refs_1_) | copy-start | bytes 589828
  83.7 16.0 %collective-permute-start.15 = (bf16[2,8,4,16,192]{4,3,2,1,0:T(8,128)(2,1)S(1)}, bf16[2,8,4,16,192]{4,3,2,1,0:T(8,128)(2,1)S(1)}, u32[]{:S(2)}, u32[]{:S(2)}) collective-permute-start(bf16[2,8,4,16,192]{4,3,2,1,0:T(8,128)(2,1)S(1)} %pad_maximum_fusion), channel_id=1, source_target_pairs={{0,32},{32,0},{1,33},{33,1},{2,34},{34,2},{3,35},{35,3},{4,36},{36... | collective-permute-start | bytes 1179656 | tf_op jit(solution)/shard_map/ppermute | solution.py:32
  99.7 5.6 %copy-start.3 = (bf16[2,8,4,16,192]{4,3,2,1,0:T(8,128)(2,1)}, bf16[2,8,4,16,192]{4,3,2,1,0:T(8,128)(2,1)S(1)}, u32[]{:S(2)}) copy-start(bf16[2,8,4,16,192]{4,3,2,1,0:T(8,128)(2,1)S(1)} %collective-permute-done.15.refs_2_) | copy-start | bytes 1179652
  105.2 39.8 %collective-permute-start.16 = (bf16[2,192,3072]{2,1,0:T(8,128)(2,1)}, bf16[2,192,3072]{2,1,0:T(8,128)(2,1)}, u32[]{:S(2)}, u32[]{:S(2)}) collective-permute-start(bf16[2,192,3072]{2,1,0:T(8,128)(2,1)} %weight_sums.3), channel_id=1, source_target_pairs={{0,1},{1,0},{2,3},{3,2},{4,5},{5,4},{6,7},{7,6},{8,9},{9,8},{10,11... | collective-permute-start | bytes 7077896 | tf_op jit(solution)/shard_map/ppermute | solution.py:32
  107.2 31.8 %copy-start = (bf16[512,3072]{1,0:T(8,128)(2,1)S(1)}, bf16[512,3072]{1,0:T(8,128)(2,1)}, u32[]{:S(2)}) copy-start(bf16[512,3072]{1,0:T(8,128)(2,1)} %get-tuple-element.35.refs_3_) | copy-start | bytes 9437188
  128.4 0.8 copy-start.5
  129.2 41.3 %all-to-all-start.2 = ((bf16[16,64,192]{2,1,0:T(8,128)(2,1)}), bf16[16,64,192]{2,1,0:T(8,128)(2,1)}, u32[]{:S(2)}, u32[]{:S(2)}) async-start(bf16[16,64,192]{2,1,0:T(8,128)(2,1)} %bitcast.15), calls=%async_computation.2 | async-start | bytes 1048576 | tf_op jit(solution)/shard_map/all_to_all | solution.py:226
  138.9 1.0 copy-start.2
  139.9 1.0 copy-start.4
  149.7 35.3 %collective-permute-start.17 = (bf16[192,3072]{1,0:T(8,128)(2,1)}, bf16[192,3072]{1,0:T(8,128)(2,1)}, u32[]{:S(2)}, u32[]{:S(2)}) collective-permute-start(bf16[192,3072]{1,0:T(8,128)(2,1)} %get-tuple-element.37), channel_id=1, source_target_pairs={{0,2},{2,0},{1,3},{3,1},{4,6},{6,4},{5,7},{7,5},{8,10},{10,8},{9,1... | collective-permute-start | bytes 3538952 | tf_op jit(solution)/shard_map/ppermute | solution.py:32

commit v5 on v4

--- a/solution.py
+++ b/solution.py
@@ -174,7 +174,6 @@
     gh = (grad_out.astype(F32) * gelu_slope(pre_act.astype(F32))).astype(BF16)
 
     part = whole_call(part_kernel, (32, 16, 192), "part")(inputs)
-    part, gh = lax.optimization_barrier((part, gh))
     part = lax.all_to_all(part, ("gx", "yl", "core"), split_axis=0, concat_axis=0, tiled=True)
     part = part.reshape(8, 4, 16, 192)
 
@@ -184,7 +183,7 @@
         far.append(across(jnp.concatenate([down[-1], up[-1]], 0)))
         down.append(hop(down[-1], -1))
         if s == 1:
-            up[2], down[2], far[0] = lax.optimization_barrier((up[2], down[2], far[0]))
+            up[2], down[2] = lax.optimization_barrier((up[2], down[2]))
         if s == 2:
             up[3], down[3], far[1], part = lax.optimization_barrier((up[3], down[3], far[1], part))
             beside_x = swap(part, "xl")

time: 190 us -> 199 us (1.047)
  the two profiles are of different devices: /device:TPU:32 before, /device:TPU:48 now
where the time goes in v5:
time: 199 us; the launch traced here: 198 us
  starting transfers between devices  86 us (43%)
  waiting for transfers between devices  42.1 us (21%)
  blocking collectives  35.7 us (18%)
  Pallas kernels  26.5 us (13%)
  local copies, waits for them, and re-layouts  3.92 us (2%)
  other arithmetic  3 us (2%)
    ppermute x7, starting transfers between devices, hop(): lax.ppermute(value, 'gx', [(RING[q], RING[(q + step) % 8]) for q in range...  25.7 us
    all_to_all x1, blocking collectives, shards(): lax.all_to_all(rows.reshape(16, 8, 16, 192), ('xp', 'xl', 'yl', 'core'),...  23.3 us
    ppermute x7, starting transfers between devices, swap(): return lax.ppermute(value, axis, [(0, 1), (1, 0)])  19.9 us
    all_to_all x1, waiting for transfers between devices, shards(): lax.all_to_all(rows.reshape(16, 64, 192), ('gx', 'zh'), split_axis=0, con...  18.5 us
    all_to_all x1, starting transfers between devices, shards(): lax.all_to_all(part, ('gx', 'yl', 'core'), split_axis=0, concat_axis=0, t...  14.7 us
    ppermute x7, waiting for transfers between devices, hop(): lax.ppermute(value, 'gx', [(RING[q], RING[(q + step) % 8]) for q in range...  14 us
    all_to_all x1, starting transfers between devices, shards(): lax.all_to_all(rows.reshape(16, 64, 192), ('gx', 'zh'), split_axis=0, con...  13.5 us
    all_to_all x1, blocking collectives, shards(): lax.all_to_all(rows, ('xp', 'xl'), split_axis=0, concat_axis=0, tiled=True)  12.4 us
  transfers between devices with their start and end apart: 20, of which 8 were waited for; matrix products, arithmetic and copies ran while one was open for 2% of the time, Pallas kernels for 9%

profile of v5, /device:TPU:48, one launch (start us, length us, event | category | flops | bytes accessed | tf_op | source)
XLA Modules:
  0.0 198.1 jit_solution(7742046286294858176)
XLA Ops:
  0.6 3.2 %collective-permute-start.2 = (bf16[192,3072]{1,0:T(8,128)(2,1)}, bf16[192,3072]{1,0:T(8,128)(2,1)}, u32[]{:S(2)}, u32[]{:S(2)}) collective-permute-start(bf16[192,3072]{1,0:T(8,128)(2,1)} %refs_12_), channel_id=1, source_target_pairs={{0,2},{2,0},{1,3},{3,1},{4,6},{6,4},{5,7},{7,5},{8,10},{10,8},{9,1... | collective-permute-start | bytes 3538952 | tf_op jit(solution)/shard_map/ppermute | solution.py:32
  7.2 5.1 %collective-permute-start.1 = (bf16[32,3072]{1,0:T(8,128)(2,1)S(1)}, bf16[32,3072]{1,0:T(8,128)(2,1)S(1)}, u32[]{:S(2)}, u32[]{:S(2)}) collective-permute-start(bf16[32,3072]{1,0:T(8,128)(2,1)S(1)} %fusion.6.refs_0_), channel_id=1, source_target_pairs={{0,64},{128,0},{256,128},{384,256},{448,384},{320,448},{192,320},{... | collective-permute-start | bytes 589832 | tf_op jit(solution)/shard_map/ppermute | solution.py:28
  12.2 2.7 %collective-permute-done.refs_1_ = bf16[32,3072]{1,0:T(8,128)(2,1)S(1)} collective-permute-done((bf16[32,3072]{1,0:T(8,128)(2,1)S(1)}, bf16[32,3072]{1,0:T(8,128)(2,1)S(1)}, u32[]{:S(2)}, u32[]{:S(2)}) %collective-permute-start) | collective-permute-done | bytes 196640 | tf_op jit(solution)/shard_map/ppermute | solution.py:28
  14.9 2.7 %collective-permute-start.3 = (bf16[32,3072]{1,0:T(8,128)(2,1)S(1)}, bf16[32,3072]{1,0:T(8,128)(2,1)S(1)}, u32[]{:S(2)}, u32[]{:S(2)}) collective-permute-start(bf16[32,3072]{1,0:T(8,128)(2,1)S(1)} %collective-permute-done.refs_1_), channel_id=1, source_target_pairs={{0,128},{128,256},{256,384},{384,448},{448,320},{320,192},{192,64}... | collective-permute-start | bytes 589832 | tf_op jit(solution)/shard_map/ppermute | solution.py:28
  19.6 14.7 %all-to-all-start = ((bf16[32,16,192]{2,1,0:T(8,128)(2,1)}), bf16[32,16,192]{2,1,0:T(8,128)(2,1)S(1)}, u32[]{:S(2)}, u32[]{:S(2)}) async-start(bf16[32,16,192]{2,1,0:T(8,128)(2,1)} %part.1), calls=%async_computation | async-start | bytes 524288 | tf_op jit(solution)/shard_map/all_to_all | solution.py:177
  34.4 4.3 %collective-permute-start.4 = (bf16[32,3072]{1,0:T(8,128)(2,1)S(1)}, bf16[32,3072]{1,0:T(8,128)(2,1)S(1)}, u32[]{:S(2)}, u32[]{:S(2)}) collective-permute-start(bf16[32,3072]{1,0:T(8,128)(2,1)S(1)} %collective-permute-done.1.refs_2_), channel_id=1, source_target_pairs={{0,64},{128,0},{256,128},{384,256},{448,384},{320,448},{192,320},{... | collective-permute-start | bytes 589832 | tf_op jit(solution)/shard_map/ppermute | solution.py:28
  39.4 2.0 %collective-permute-start.7 = (bf16[64,3072]{1,0:T(8,128)(2,1)}, bf16[64,3072]{1,0:T(8,128)(2,1)S(1)}, u32[]{:S(2)}, u32[]{:S(2)}) collective-permute-start(bf16[64,3072]{1,0:T(8,128)(2,1)} %pad_maximum_fusion.1), channel_id=1, source_target_pairs={{0,6},{2,4},{4,2},{6,0},{1,7},{3,5},{5,3},{7,1},{8,14},{10,12},{12... | collective-permute-start | bytes 1179656 | tf_op jit(solution)/shard_map/ppermute | solution.py:36
  41.5 6.0 %collective-permute-done.4.refs_4_ = bf16[32,3072]{1,0:T(8,128)(2,1)S(1)} collective-permute-done((bf16[32,3072]{1,0:T(8,128)(2,1)S(1)}, bf16[32,3072]{1,0:T(8,128)(2,1)S(1)}, u32[]{:S(2)}, u32[]{:S(2)}) %collective-permute-start.4) | collective-permute-done | bytes 196640 | tf_op jit(solution)/shard_map/ppermute | solution.py:28
  47.4 3.9 %collective-permute-start.5 = (bf16[32,3072]{1,0:T(8,128)(2,1)S(1)}, bf16[32,3072]{1,0:T(8,128)(2,1)S(1)}, u32[]{:S(2)}, u32[]{:S(2)}) collective-permute-start(bf16[32,3072]{1,0:T(8,128)(2,1)S(1)} %collective-permute-done.3.refs_3_), channel_id=1, source_target_pairs={{0,128},{128,256},{256,384},{384,448},{448,320},{320,192},{192,64}... | collective-permute-start | bytes 589832 | tf_op jit(solution)/shard_map/ppermute | solution.py:28
  51.4 5.2 %collective-permute-start.6 = (bf16[32,3072]{1,0:T(8,128)(2,1)S(1)}, bf16[32,3072]{1,0:T(8,128)(2,1)S(1)}, u32[]{:S(2)}, u32[]{:S(2)}) collective-permute-start(bf16[32,3072]{1,0:T(8,128)(2,1)S(1)} %collective-permute-done.4.refs_4_), channel_id=1, source_target_pairs={{0,64},{128,0},{256,128},{384,256},{448,384},{320,448},{192,320},{... | collective-permute-start | bytes 589832 | tf_op jit(solution)/shard_map/ppermute | solution.py:28
  58.5 2.4 %collective-permute-start.13 = (bf16[192,3072]{1,0:T(8,128)(2,1)}, bf16[192,3072]{1,0:T(8,128)(2,1)}, u32[]{:S(2)}, u32[]{:S(2)}) collective-permute-start(bf16[192,3072]{1,0:T(8,128)(2,1)} %collective-permute-done.2.refs_13_), channel_id=1, source_target_pairs={{0,1},{1,0},{2,3},{3,2},{4,5},{5,4},{6,7},{7,6},{8,9},{9,8},{10,11... | collective-permute-start | bytes 3538952 | tf_op jit(solution)/shard_map/ppermute | solution.py:32
  61.7 2.2 %collective-permute-start.9 = (bf16[64,3072]{1,0:T(8,128)(2,1)}, bf16[64,3072]{1,0:T(8,128)(2,1)}, u32[]{:S(2)}, u32[]{:S(2)}) collective-permute-start(bf16[64,3072]{1,0:T(8,128)(2,1)} %pad_maximum_fusion.2), channel_id=1, source_target_pairs={{0,6},{2,4},{4,2},{6,0},{1,7},{3,5},{5,3},{7,1},{8,14},{10,12},{12... | collective-permute-start | bytes 1179656 | tf_op jit(solution)/shard_map/ppermute | solution.py:36
  63.9 3.1 %collective-permute-done.6.refs_6_ = bf16[32,3072]{1,0:T(8,128)(2,1)S(1)} collective-permute-done((bf16[32,3072]{1,0:T(8,128)(2,1)S(1)}, bf16[32,3072]{1,0:T(8,128)(2,1)S(1)}, u32[]{:S(2)}, u32[]{:S(2)}) %collective-permute-start.6) | collective-permute-done | bytes 196640 | tf_op jit(solution)/shard_map/ppermute | solution.py:28
  67.0 2.5 %collective-permute-start.8 = (bf16[32,3072]{1,0:T(8,128)(2,1)S(1)}, bf16[32,3072]{1,0:T(8,128)(2,1)S(1)}, u32[]{:S(2)}, u32[]{:S(2)}) collective-permute-start(bf16[32,3072]{1,0:T(8,128)(2,1)S(1)} %collective-permute-done.5.refs_5_), channel_id=1, source_target_pairs={{0,128},{128,256},{256,384},{384,448},{448,320},{320,192},{192,64}... | collective-permute-start | bytes 589832 | tf_op jit(solution)/shard_map/ppermute | solution.py:28
  69.5 3.7 %collective-permute-start.10 = (bf16[64,3072]{1,0:T(8,128)(2,1)S(1)}, bf16[64,3072]{1,0:T(8,128)(2,1)S(1)}, u32[]{:S(2)}, u32[]{:S(2)}) collective-permute-start(bf16[64,3072]{1,0:T(8,128)(2,1)S(1)} %pad_maximum_fusion.3), channel_id=1, source_target_pairs={{0,6},{2,4},{4,2},{6,0},{1,7},{3,5},{5,3},{7,1},{8,14},{10,12},{12... | collective-permute-start | bytes 1179656 | tf_op jit(solution)/shard_map/ppermute | solution.py:36
  73.2 2.2 %collective-permute-done.8.refs_7_ = bf16[32,3072]{1,0:T(8,128)(2,1)S(1)} collective-permute-done((bf16[32,3072]{1,0:T(8,128)(2,1)S(1)}, bf16[32,3072]{1,0:T(8,128)(2,1)S(1)}, u32[]{:S(2)}, u32[]{:S(2)}) %collective-permute-start.8) | collective-permute-done | bytes 196640 | tf_op jit(solution)/shard_map/ppermute | solution.py:28
  75.4 3.4 %collective-permute-start.14 = (bf16[8,4,16,192]{3,2,1,0:T(8,128)(2,1)S(1)}, bf16[8,4,16,192]{3,2,1,0:T(8,128)(2,1)S(1)}, u32[]{:S(2)}, u32[]{:S(2)}) collective-permute-start(bf16[8,4,16,192]{3,2,1,0:T(8,128)(2,1)S(1)} %bitcast.8), channel_id=1, source_target_pairs={{0,16},{16,0},{1,17},{17,1},{2,18},{18,2},{3,19},{19,3},{4,20},{20... | collective-permute-start | bytes 589832 | tf_op jit(solution)/shard_map/ppermute | solution.py:32
  78.9 4.8 %collective-permute-done.14.refs_1_ = bf16[8,4,16,192]{3,2,1,0:T(8,128)(2,1)S(1)} collective-permute-done((bf16[8,4,16,192]{3,2,1,0:T(8,128)(2,1)S(1)}, bf16[8,4,16,192]{3,2,1,0:T(8,128)(2,1)S(1)}, u32[]{:S(2)}, u32[]{:S(2)}) %collective-permute-start.14) | collective-permute-done | bytes 196640 | tf_op jit(solution)/shard_map/ppermute | solution.py:32
  83.7 4.4 %collective-permute-start.11 = (bf16[64,3072]{1,0:T(8,128)(2,1)S(1)}, bf16[64,3072]{1,0:T(8,128)(2,1)S(1)}, u32[]{:S(2)}, u32[]{:S(2)}) collective-permute-start(bf16[64,3072]{1,0:T(8,128)(2,1)S(1)} %pad_maximum_fusion.4), channel_id=1, source_target_pairs={{0,6},{2,4},{4,2},{6,0},{1,7},{3,5},{5,3},{7,1},{8,14},{10,12},{12... | collective-permute-start | bytes 1179656 | tf_op jit(solution)/shard_map/ppermute | solution.py:36
  88.2 4.7 %collective-permute-start.15 = (bf16[2,8,4,16,192]{4,3,2,1,0:T(8,128)(2,1)S(1)}, bf16[2,8,4,16,192]{4,3,2,1,0:T(8,128)(2,1)S(1)}, u32[]{:S(2)}, u32[]{:S(2)}) collective-permute-start(bf16[2,8,4,16,192]{4,3,2,1,0:T(8,128)(2,1)S(1)} %pad_maximum_fusion), channel_id=1, source_target_pairs={{0,32},{32,0},{1,33},{33,1},{2,34},{34,2},{3,35},{35,3},{4,36},{36... | collective-permute-start | bytes 1179656 | tf_op jit(solution)/shard_map/ppermute | solution.py:32
  93.0 2.6 %collective-permute-done.11.refs_11_ = bf16[64,3072]{1,0:T(8,128)(2,1)S(1)} collective-permute-done((bf16[64,3072]{1,0:T(8,128)(2,1)S(1)}, bf16[64,3072]{1,0:T(8,128)(2,1)S(1)}, u32[]{:S(2)}, u32[]{:S(2)}) %collective-permute-start.11) | collective-permute-done | bytes 393248 | tf_op jit(solution)/shard_map/ppermute | solution.py:36
  95.6 5.6 %products.1 = (bf16[4,4,8,16,192]{4,3,2,1,0:T(8,128)(2,1)S(1)}, bf16[512,3072]{1,0:T(8,128)(2,1)}) custom-call(bf16[32,3072]{1,0:T(8,128)(2,1)S(1)} %fusion.6.refs_0_, bf16[32,3072]{1,0:T(8,128)(2,1)S(1)} %collective-permute-done.refs_1_, bf16[32,3072]{1,0:T(8,128)(2,1)S(1)} %collective-permute-done.1.refs_2_, ...), custom_call_target="tpu_custom_call" | custom-call | flops 2415919104 | bytes 12582912 | tf_op jit(solution)/shard_map/products/pallas_call | solution.py:198
  101.2 2.2 %collective-permute-done.15.refs_2_ = bf16[2,8,4,16,192]{4,3,2,1,0:T(8,128)(2,1)S(1)} collective-permute-done((bf16[2,8,4,16,192]{4,3,2,1,0:T(8,128)(2,1)S(1)}, bf16[2,8,4,16,192]{4,3,2,1,0:T(8,128)(2,1)S(1)}, u32[]{:S(2)}, u32[]{:S(2)}) %collective-permute-start.15) | collective-permute-done | bytes 393248 | tf_op jit(solution)/shard_map/ppermute | solution.py:32
  103.4 5.6 %weight_sums.3 = bf16[2,192,3072]{2,1,0:T(8,128)(2,1)} custom-call(bf16[8,4,16,192]{3,2,1,0:T(8,128)(2,1)S(1)} %bitcast.10, bf16[8,4,16,192]{3,2,1,0:T(8,128)(2,1)S(1)} %collective-permute-done.14.refs_1_, bf16[2,8,4,16,192]{4,3,2,1,0:T(8,128)(2,1)S(1)} %collective-permute-done.15.refs_2_, bf16[512,3072]{1,0:T(8,128)(2,1)} %get-tuple-element.29.refs_3_), custom_call_target="tpu_custom_call" | custom-call | flops 1207959552 | bytes 8388608 | tf_op jit(solution)/shard_map/weight_sums/pallas_call | solution.py:107
  110.9 23.3 %all_to_all.20 = bf16[16,8,16,192]{3,2,1,0:T(8,128)(2,1)S(1)} all-to-all(bf16[16,8,16,192]{3,2,1,0:T(8,128)(2,1)S(1)} %bitcast.16), channel_id=1, replica_groups=mesh['gx'=8,'xp'=2,'xl'=2,'zh'=2,'yp'=2,'yl'=2,'core'=2] {'xp','xl','yl'..., dimensions={0} | all-to-all | bytes 1572864 | tf_op jit(solution)/shard_map/all_to_all | solution.py:215
  135.1 13.5 %all-to-all-start.2 = ((bf16[16,64,192]{2,1,0:T(8,128)(2,1)}), bf16[16,64,192]{2,1,0:T(8,128)(2,1)}, u32[]{:S(2)}, u32[]{:S(2)}) async-start(bf16[16,64,192]{2,1,0:T(8,128)(2,1)} %bitcast.15), calls=%async_computation.2 | async-start | bytes 1048576 | tf_op jit(solution)/shard_map/all_to_all | solution.py:225
  150.6 4.1 %weight_sums.2.keep = f32[2,192,3072]{2,1,0:T(8,128)} custom-call(bf16[8,4,16,192]{3,2,1,0:T(8,128)(2,1)S(1)} %bitcast.11, bf16[8,4,16,192]{3,2,1,0:T(8,128)(2,1)S(1)} %copy-done.2, bf16[2,8,4,16,192]{4,3,2,1,0:T(8,128)(2,1)S(1)} %copy-done.4, bf16[512,3072]{1,0:T(8,128)(2,1)S(1)} %copy-done), custom_call_target="tpu_custom_call" | custom-call | flops 1207959552 | bytes 8388608 | tf_op jit(solution)/shard_map/weight_sums/pallas_call | solution.py:107
  154.7 4.7 %meet.1 = (f32[192,3072]{1,0:T(8,128)S(1)}, bf16[192,3072]{1,0:T(8,128)(2,1)}) custom-call(f32[2,192,3072]{2,1,0:T(8,128)} %weight_sums.2.keep, bf16[2,192,3072]{2,1,0:T(8,128)(2,1)} %collective-permute-done.16.met), custom_call_target="tpu_custom_call" | custom-call | tf_op jit(solution)/shard_map/meet/pallas_call | solution.py:235
  159.3 2.3 %collective-permute-start.17 = (bf16[192,3072]{1,0:T(8,128)(2,1)}, bf16[192,3072]{1,0:T(8,128)(2,1)}, u32[]{:S(2)}, u32[]{:S(2)}) collective-permute-start(bf16[192,3072]{1,0:T(8,128)(2,1)} %get-tuple-element.31), channel_id=1, source_target_pairs={{0,2},{2,0},{1,3},{3,1},{4,6},{6,4},{5,7},{7,5},{8,10},{10,8},{9,1... | collective-permute-start | bytes 3538952 | tf_op jit(solution)/shard_map/ppermute | solution.py:32
  161.6 18.5 %all-to-all-done.2 = bf16[16,64,192]{2,1,0:T(8,128)(2,1)} async-done(((bf16[16,64,192]{2,1,0:T(8,128)(2,1)}), bf16[16,64,192]{2,1,0:T(8,128)(2,1)}, u32[]{:S(2)}, u32[]{:S(2)}) %all-to-all-start.2) | async-done | bytes 393248 | tf_op jit(solution)/shard_map/all_to_all | solution.py:225
  181.3 12.4 %all_to_all.21 = bf16[4,64,1536]{2,1,0:T(8,128)(2,1)S(1)} all-to-all(bf16[4,64,1536]{2,1,0:T(8,128)(2,1)S(1)} %sum_z.1), channel_id=1, replica_groups=mesh['gx'=8,'xp'=2,'xl'=2,'zh'=2,'yp'=2,'yl'=2,'core'=2] {'xp','xl'}, dimensions={0} | all-to-all | bytes 1572864 | tf_op jit(solution)/shard_map/all_to_all | solution.py:229
  194.6 3.5 %close.1 = bf16[192,3072]{1,0:T(8,128)(2,1)} custom-call(f32[192,3072]{1,0:T(8,128)S(1)} %get-tuple-element.30.own, bf16[192,3072]{1,0:T(8,128)(2,1)} %collective-permute-done.17.passed), custom_call_target="tpu_custom_call" | custom-call | tf_op jit(solution)/shard_map/close/pallas_call | solution.py:247
  (41 shorter events, 15.8 us)
Async XLA Ops:
  0.6 55.9 %collective-permute-start.2 = (bf16[192,3072]{1,0:T(8,128)(2,1)}, bf16[192,3072]{1,0:T(8,128)(2,1)}, u32[]{:S(2)}, u32[]{:S(2)}) collective-permute-start(bf16[192,3072]{1,0:T(8,128)(2,1)} %refs_12_), channel_id=1, source_target_pairs={{0,2},{2,0},{1,3},{3,1},{4,6},{6,4},{5,7},{7,5},{8,10},{10,8},{9,1... | collective-permute-start | bytes 3538952 | tf_op jit(solution)/shard_map/ppermute | solution.py:32
  5.1 9.8 %collective-permute-start = (bf16[32,3072]{1,0:T(8,128)(2,1)S(1)}, bf16[32,3072]{1,0:T(8,128)(2,1)S(1)}, u32[]{:S(2)}, u32[]{:S(2)}) collective-permute-start(bf16[32,3072]{1,0:T(8,128)(2,1)S(1)} %fusion.6.refs_0_), channel_id=1, source_target_pairs={{0,128},{128,256},{256,384},{384,448},{448,320},{320,192},{192,64}... | collective-permute-start | bytes 589832 | tf_op jit(solution)/shard_map/ppermute | solution.py:28
  7.2 27.2 %collective-permute-start.1 = (bf16[32,3072]{1,0:T(8,128)(2,1)S(1)}, bf16[32,3072]{1,0:T(8,128)(2,1)S(1)}, u32[]{:S(2)}, u32[]{:S(2)}) collective-permute-start(bf16[32,3072]{1,0:T(8,128)(2,1)S(1)} %fusion.6.refs_0_), channel_id=1, source_target_pairs={{0,64},{128,0},{256,128},{384,256},{448,384},{320,448},{192,320},{... | collective-permute-start | bytes 589832 | tf_op jit(solution)/shard_map/ppermute | solution.py:28
  14.9 23.7 %collective-permute-start.3 = (bf16[32,3072]{1,0:T(8,128)(2,1)S(1)}, bf16[32,3072]{1,0:T(8,128)(2,1)S(1)}, u32[]{:S(2)}, u32[]{:S(2)}) collective-permute-start(bf16[32,3072]{1,0:T(8,128)(2,1)S(1)} %collective-permute-done.refs_1_), channel_id=1, source_target_pairs={{0,128},{128,256},{256,384},{384,448},{448,320},{320,192},{192,64}... | collective-permute-start | bytes 589832 | tf_op jit(solution)/shard_map/ppermute | solution.py:28
  17.7 1.1 copy-start.6
  18.8 37.8 %copy-start.7 = (bf16[192,3072]{1,0:T(8,128)(2,1)S(1)}, bf16[192,3072]{1,0:T(8,128)(2,1)}, u32[]{:S(2)}) copy-start(bf16[192,3072]{1,0:T(8,128)(2,1)} %refs_12_) | copy-start | bytes 3538948
  19.6 47.4 %all-to-all-start = ((bf16[32,16,192]{2,1,0:T(8,128)(2,1)}), bf16[32,16,192]{2,1,0:T(8,128)(2,1)S(1)}, u32[]{:S(2)}, u32[]{:S(2)}) async-start(bf16[32,16,192]{2,1,0:T(8,128)(2,1)} %part.1), calls=%async_computation | async-start | bytes 524288 | tf_op jit(solution)/shard_map/all_to_all | solution.py:177
  34.4 13.1 %collective-permute-start.4 = (bf16[32,3072]{1,0:T(8,128)(2,1)S(1)}, bf16[32,3072]{1,0:T(8,128)(2,1)S(1)}, u32[]{:S(2)}, u32[]{:S(2)}) collective-permute-start(bf16[32,3072]{1,0:T(8,128)(2,1)S(1)} %collective-permute-done.1.refs_2_), channel_id=1, source_target_pairs={{0,64},{128,0},{256,128},{384,256},{448,384},{320,448},{192,320},{... | collective-permute-start | bytes 589832 | tf_op jit(solution)/shard_map/ppermute | solution.py:28
  39.4 27.5 %collective-permute-start.7 = (bf16[64,3072]{1,0:T(8,128)(2,1)}, bf16[64,3072]{1,0:T(8,128)(2,1)S(1)}, u32[]{:S(2)}, u32[]{:S(2)}) collective-permute-start(bf16[64,3072]{1,0:T(8,128)(2,1)} %pad_maximum_fusion.1), channel_id=1, source_target_pairs={{0,6},{2,4},{4,2},{6,0},{1,7},{3,5},{5,3},{7,1},{8,14},{10,12},{12... | collective-permute-start | bytes 1179656 | tf_op jit(solution)/shard_map/ppermute | solution.py:36
  47.4 14.3 %collective-permute-start.5 = (bf16[32,3072]{1,0:T(8,128)(2,1)S(1)}, bf16[32,3072]{1,0:T(8,128)(2,1)S(1)}, u32[]{:S(2)}, u32[]{:S(2)}) collective-permute-start(bf16[32,3072]{1,0:T(8,128)(2,1)S(1)} %collective-permute-done.3.refs_3_), channel_id=1, source_target_pairs={{0,128},{128,256},{256,384},{384,448},{448,320},{320,192},{192,64}... | collective-permute-start | bytes 589832 | tf_op jit(solution)/shard_map/ppermute | solution.py:28
  51.4 15.6 %collective-permute-start.6 = (bf16[32,3072]{1,0:T(8,128)(2,1)S(1)}, bf16[32,3072]{1,0:T(8,128)(2,1)S(1)}, u32[]{:S(2)}, u32[]{:S(2)}) collective-permute-start(bf16[32,3072]{1,0:T(8,128)(2,1)S(1)} %collective-permute-done.4.refs_4_), channel_id=1, source_target_pairs={{0,64},{128,0},{256,128},{384,256},{448,384},{320,448},{192,320},{... | collective-permute-start | bytes 589832 | tf_op jit(solution)/shard_map/ppermute | solution.py:28
  56.6 39.0 %collective-permute-start.12 = (bf16[192,3072]{1,0:T(8,128)(2,1)S(1)}, bf16[192,3072]{1,0:T(8,128)(2,1)}, u32[]{:S(2)}, u32[]{:S(2)}) collective-permute-start(bf16[192,3072]{1,0:T(8,128)(2,1)S(1)} %copy-done.7), channel_id=1, source_target_pairs={{0,1},{1,0},{2,3},{3,2},{4,5},{5,4},{6,7},{7,6},{8,9},{9,8},{10,11... | collective-permute-start | bytes 3538952 | tf_op jit(solution)/shard_map/ppermute | solution.py:32
  58.5 37.1 %collective-permute-start.13 = (bf16[192,3072]{1,0:T(8,128)(2,1)}, bf16[192,3072]{1,0:T(8,128)(2,1)}, u32[]{:S(2)}, u32[]{:S(2)}) collective-permute-start(bf16[192,3072]{1,0:T(8,128)(2,1)} %collective-permute-done.2.refs_13_), channel_id=1, source_target_pairs={{0,1},{1,0},{2,3},{3,2},{4,5},{5,4},{6,7},{7,6},{8,9},{9,8},{10,11... | collective-permute-start | bytes 3538952 | tf_op jit(solution)/shard_map/ppermute | solution.py:32
  61.7 26.5 %collective-permute-start.9 = (bf16[64,3072]{1,0:T(8,128)(2,1)}, bf16[64,3072]{1,0:T(8,128)(2,1)}, u32[]{:S(2)}, u32[]{:S(2)}) collective-permute-start(bf16[64,3072]{1,0:T(8,128)(2,1)} %pad_maximum_fusion.2), channel_id=1, source_target_pairs={{0,6},{2,4},{4,2},{6,0},{1,7},{3,5},{5,3},{7,1},{8,14},{10,12},{12... | collective-permute-start | bytes 1179656 | tf_op jit(solution)/shard_map/ppermute | solution.py:36
  67.0 8.5 %collective-permute-start.8 = (bf16[32,3072]{1,0:T(8,128)(2,1)S(1)}, bf16[32,3072]{1,0:T(8,128)(2,1)S(1)}, u32[]{:S(2)}, u32[]{:S(2)}) collective-permute-start(bf16[32,3072]{1,0:T(8,128)(2,1)S(1)} %collective-permute-done.5.refs_5_), channel_id=1, source_target_pairs={{0,128},{128,256},{256,384},{384,448},{448,320},{320,192},{192,64}... | collective-permute-start | bytes 589832 | tf_op jit(solution)/shard_map/ppermute | solution.py:28
  69.5 23.4 %collective-permute-start.10 = (bf16[64,3072]{1,0:T(8,128)(2,1)S(1)}, bf16[64,3072]{1,0:T(8,128)(2,1)S(1)}, u32[]{:S(2)}, u32[]{:S(2)}) collective-permute-start(bf16[64,3072]{1,0:T(8,128)(2,1)S(1)} %pad_maximum_fusion.3), channel_id=1, source_target_pairs={{0,6},{2,4},{4,2},{6,0},{1,7},{3,5},{5,3},{7,1},{8,14},{10,12},{12... | collective-permute-start | bytes 1179656 | tf_op jit(solution)/shard_map/ppermute | solution.py:36
  75.4 8.3 %collective-permute-start.14 = (bf16[8,4,16,192]{3,2,1,0:T(8,128)(2,1)S(1)}, bf16[8,4,16,192]{3,2,1,0:T(8,128)(2,1)S(1)}, u32[]{:S(2)}, u32[]{:S(2)}) collective-permute-start(bf16[8,4,16,192]{3,2,1,0:T(8,128)(2,1)S(1)} %bitcast.8), channel_id=1, source_target_pairs={{0,16},{16,0},{1,17},{17,1},{2,18},{18,2},{3,19},{19,3},{4,20},{20... | collective-permute-start | bytes 589832 | tf_op jit(solution)/shard_map/ppermute | solution.py:32
  83.7 19.7 %copy-start.1 = (bf16[8,4,16,192]{3,2,1,0:T(8,128)(2,1)}, bf16[8,4,16,192]{3,2,1,0:T(8,128)(2,1)S(1)}, u32[]{:S(2)}) copy-start(bf16[8,4,16,192]{3,2,1,0:T(8,128)(2,1)S(1)} %collective-permute-done.14.refs_1_) | copy-start | bytes 589828
  83.7 11.9 %collective-permute-start.11 = (bf16[64,3072]{1,0:T(8,128)(2,1)S(1)}, bf16[64,3072]{1,0:T(8,128)(2,1)S(1)}, u32[]{:S(2)}, u32[]{:S(2)}) collective-permute-start(bf16[64,3072]{1,0:T(8,128)(2,1)S(1)} %pad_maximum_fusion.4), channel_id=1, source_target_pairs={{0,6},{2,4},{4,2},{6,0},{1,7},{3,5},{5,3},{7,1},{8,14},{10,12},{12... | collective-permute-start | bytes 1179656 | tf_op jit(solution)/shard_map/ppermute | solution.py:36
  88.2 15.2 %collective-permute-start.15 = (bf16[2,8,4,16,192]{4,3,2,1,0:T(8,128)(2,1)S(1)}, bf16[2,8,4,16,192]{4,3,2,1,0:T(8,128)(2,1)S(1)}, u32[]{:S(2)}, u32[]{:S(2)}) collective-permute-start(bf16[2,8,4,16,192]{4,3,2,1,0:T(8,128)(2,1)S(1)} %pad_maximum_fusion), channel_id=1, source_target_pairs={{0,32},{32,0},{1,33},{33,1},{2,34},{34,2},{3,35},{35,3},{4,36},{36... | collective-permute-start | bytes 1179656 | tf_op jit(solution)/shard_map/ppermute | solution.py:32
  103.4 5.6 %copy-start.3 = (bf16[2,8,4,16,192]{4,3,2,1,0:T(8,128)(2,1)}, bf16[2,8,4,16,192]{4,3,2,1,0:T(8,128)(2,1)S(1)}, u32[]{:S(2)}) copy-start(bf16[2,8,4,16,192]{4,3,2,1,0:T(8,128)(2,1)S(1)} %collective-permute-done.15.refs_2_) | copy-start | bytes 1179652
  109.0 45.7 %collective-permute-start.16 = (bf16[2,192,3072]{2,1,0:T(8,128)(2,1)}, bf16[2,192,3072]{2,1,0:T(8,128)(2,1)}, u32[]{:S(2)}, u32[]{:S(2)}) collective-permute-start(bf16[2,192,3072]{2,1,0:T(8,128)(2,1)} %weight_sums.3), channel_id=1, source_target_pairs={{0,1},{1,0},{2,3},{3,2},{4,5},{5,4},{6,7},{7,6},{8,9},{9,8},{10,11... | collective-permute-start | bytes 7077896 | tf_op jit(solution)/shard_map/ppermute | solution.py:32
  110.9 37.7 %copy-start = (bf16[512,3072]{1,0:T(8,128)(2,1)S(1)}, bf16[512,3072]{1,0:T(8,128)(2,1)}, u32[]{:S(2)}) copy-start(bf16[512,3072]{1,0:T(8,128)(2,1)} %get-tuple-element.29.refs_3_) | copy-start | bytes 9437188
  134.3 0.8 copy-start.5
  135.1 45.0 %all-to-all-start.2 = ((bf16[16,64,192]{2,1,0:T(8,128)(2,1)}), bf16[16,64,192]{2,1,0:T(8,128)(2,1)}, u32[]{:S(2)}, u32[]{:S(2)}) async-start(bf16[16,64,192]{2,1,0:T(8,128)(2,1)} %bitcast.15), calls=%async_computation.2 | async-start | bytes 1048576 | tf_op jit(solution)/shard_map/all_to_all | solution.py:225
  148.6 1.0 copy-start.2
  149.5 1.0 copy-start.4
  159.3 35.3 %collective-permute-start.17 = (bf16[192,3072]{1,0:T(8,128)(2,1)}, bf16[192,3072]{1,0:T(8,128)(2,1)}, u32[]{:S(2)}, u32[]{:S(2)}) collective-permute-start(bf16[192,3072]{1,0:T(8,128)(2,1)} %get-tuple-element.31), channel_id=1, source_target_pairs={{0,2},{2,0},{1,3},{3,1},{4,6},{6,4},{5,7},{7,5},{8,10},{10,8},{9,1... | collective-permute-start | bytes 3538952 | tf_op jit(solution)/shard_map/ppermute | solution.py:32
